TPU v7x, 32 devices: a whole 2x2x4 slice. The times are simulated.
32 devices in a mesh: seq: 8 (over z, y), ch: 4 (over x, core).
Axes of the slice: x: 2, y: 2, z: 4, core: 2. Of those that a mesh axis runs over, the one named last changes fastest.
Arguments:
- inputs: bfloat16 [512, 512, 1024], P('seq', None, 'ch'), may hold values from -6 to 6
- cotangent: bfloat16 [512, 512, 1024], P(None, 'seq', 'ch'), may hold values from -6 to 6
- right_weight: bfloat16 [512, 512], replicated, may hold values from -0.25 to 0.25
- left_weight: bfloat16 [512, 512], replicated, may hold values from -0.25 to 0.25
- first_gate: bfloat16 [512, 1024], P(None, 'ch'), may hold values from -4 to 4
- second_gate: bfloat16 [512, 1024], P(None, 'ch'), may hold values from -4 to 4
Outputs:
- output: bfloat16 [512, 512, 1024], P(None, 'seq', 'ch')
- grad_inputs: bfloat16 [512, 512, 1024], P('seq', None, 'ch')
- grad_right: float32 [512, 512], P(('seq', 'ch'))
- grad_left: float32 [512, 512], P(('seq', 'ch'))
- grad_first_gate: float32 [512, 1024], P('seq', 'ch')
- grad_second_gate: float32 [512, 1024], P('seq', 'ch')
All inputs are finite; a program needn't handle non-finite values.
Results may differ from a plain program's by a relative error of at most 0.015.
Values may be sent and summed in bfloat16 or wider, within the bound.
No kernel may reach another device: no remote copies, remote signals or barrier semaphores. Data moves between devices by JAX's collectives and lax.ppermute only.
A program may use at most 256 MiB of HBM per device.

v0:
```python
import jax
import jax.numpy as jnp
from jax import lax
from jax.sharding import PartitionSpec as P


def per_device(inputs, cotangent, right_weight, left_weight, first_gate, second_gate):
    section_one = jnp.einsum(
        "kj,ijd->ikd", right_weight, inputs, preferred_element_type=jnp.float32
    ).astype(jnp.bfloat16)
    gate_one = first_gate.astype(jnp.float32)[None, :, :]
    panels = (section_one.astype(jnp.float32) * gate_one).astype(jnp.bfloat16)
    received = lax.all_to_all(panels, "seq", split_axis=1, concat_axis=0, tiled=True)
    mixed = jnp.einsum("mi,ikd->mkd", left_weight, received, preferred_element_type=jnp.float32)
    logistic = jax.nn.sigmoid(mixed)
    activated = mixed * logistic
    gate_two = second_gate.astype(jnp.float32)[:, None, :]
    output = (activated * gate_two).astype(jnp.bfloat16)
    grad_out = cotangent.astype(jnp.float32)
    second_part = jnp.sum(grad_out * activated, axis=1)
    grad_mixed = (grad_out * gate_two * logistic * (1.0 + mixed * (1.0 - logistic))).astype(
        jnp.bfloat16
    )
    grad_left = lax.psum_scatter(
        jnp.einsum("mkd,ikd->mi", grad_mixed, received, preferred_element_type=jnp.float32),
        ("seq", "ch"),
        scatter_dimension=0,
        tiled=True,
    )
    grad_panels = jnp.einsum(
        "mi,mkd->ikd", left_weight, grad_mixed, preferred_element_type=jnp.float32
    ).astype(jnp.bfloat16)
    returned = lax.all_to_all(grad_panels, "seq", split_axis=0, concat_axis=1, tiled=True)
    returned32 = returned.astype(jnp.float32)
    first_part = jnp.sum(returned32 * section_one.astype(jnp.float32), axis=0)
    grad_section = (returned32 * gate_one).astype(jnp.bfloat16)
    grad_inputs = jnp.einsum(
        "kj,ikd->ijd", right_weight, grad_section, preferred_element_type=jnp.float32
    ).astype(jnp.bfloat16)
    grad_right = lax.psum_scatter(
        jnp.einsum("ikd,ijd->kj", grad_section, inputs, preferred_element_type=jnp.float32),
        ("seq", "ch"),
        scatter_dimension=0,
        tiled=True,
    )
    grad_first, grad_second = (
        lax.psum_scatter(first_part, "seq", scatter_dimension=0, tiled=True),
        lax.psum_scatter(second_part, "seq", scatter_dimension=0, tiled=True),
    )
    return (output, grad_inputs, grad_right, grad_left, grad_first, grad_second)


def solution(mesh):
    placed = (P("seq", None, "ch"), P(None, "seq", "ch"), P(), P(), P(None, "ch"), P(None, "ch"))
    return jax.shard_map(
        per_device,
        mesh=mesh,
        in_specs=placed,
        out_specs=(
            P(None, "seq", "ch"),
            P("seq", None, "ch"),
            P(("seq", "ch"), None),
            P(("seq", "ch"), None),
            P("seq", "ch"),
            P("seq", "ch"),
        ),
        check_vma=False,
    )
```

profile of v0, /device:TPU:0, one launch (start us, length us, event | category | flops | bytes accessed | tf_op | source)
XLA Modules:
  0.0 1237.3 jit_solution(7403387252276431120)
XLA Ops:
  7.2 0.0 copy-start
  7.2 1.1 copy.59
  8.3 0.0 copy-start.2
  8.3 19.8 %fusion.8 = (bf16[64,512,256]{1,2,0:T(8,128)(2,1)}, bf16[64,256,512]{2,1,0:T(8,128)(2,1)}) fusion(f32[512,256]{0,1:T(8,128)S(1)} %copy.59, bf16[64,512,256]{2,1,0:T(8,128)(2,1)} %param.6, bf16[512,512]{1,0:T(8,128)(2,1)} %param.8), kind=kOutput, calls=%fused_computation.16 | convolution fusion | flops 8623489024 | bytes 51380224 | tf_op jit(solution)/shard_map/kj,ijd->ikd/dot_general | solution.py:8
  28.1 0.0 copy-done.2
  28.1 23.2 %copy.60 = bf16[64,512,256]{2,0,1:T(8,128)(2,1)} copy(bf16[64,512,256]{1,2,0:T(8,128)(2,1)} %get-tuple-element.33) | data formatting | bytes 33554432 | tf_op jit(solution)/shard_map/convert_element_type | solution.py:12
  51.4 0.0 copy-start.5
  51.4 7.6 all-to-all-start
  59.0 0.0 copy-done.5
  59.0 0.1 copy.64
  59.2 24.7 %copy.65 = bf16[512,64,256]{0,2,1:T(8,128)(2,1)} copy(bf16[512,64,256]{2,1,0:T(8,128)(2,1)} %param.7) | data formatting | bytes 33554432 | tf_op args[1]
  83.9 338.1 %all-to-all-done = bf16[64,512,256]{2,0,1:T(8,128)(2,1)} async-done(((bf16[64,512,256]{2,0,1:T(8,128)(2,1)}), bf16[64,512,256]{2,0,1:T(8,128)(2,1)}, u32[]{:S(2)}, u32[]{:S(2)}) %all-to-all-start) | async-done | bytes 16777248 | tf_op jit(solution)/shard_map/all_to_all | solution.py:13
  422.0 17.8 %copy.62 = bf16[8,64,64,256]{3,2,1,0:T(8,128)(2,1)} copy(bf16[8,64,64,256]{3,1,2,0:T(8,128)(2,1)} %bitcast.4) | data formatting | bytes 33554432 | tf_op jit(solution)/shard_map/all_to_all | solution.py:13
  439.8 0.0 copy-done
  439.8 39.4 %fusion.3 = (f32[512,256]{0,1:T(8,128)S(1)}, bf16[512,64,256]{0,2,1:T(8,128)(2,1)}, bf16[512,64,256]{0,2,1:T(8,128)(2,1)}) fusion(bf16[512,64,256]{0,2,1:T(8,128)(2,1)} %copy.65, f32[512,256]{0,1:T(8,128)S(1)} %copy.64, bf16[512,512]{1,0:T(8,128)(2,1)S(1)} %copy-done, bf16[512,64,256]{2,1,0:T(8,128)(2,1)} %bitcast.67), kind=kOutput, calls=%fused_computation.5 | convolution fusion | flops 8724021248 | bytes 68681728 | tf_op jit(solution)/shard_map/mi,ikd->mkd/dot_general | solution.py:14
  479.2 18.6 %convert_bitcast_fusion.2 = bf16[512,64,256]{0,2,1:T(8,128)(2,1)} fusion(bf16[512,64,256]{0,2,1:T(8,128)(2,1)} %get-tuple-element.31, bf16[512,512]{1,0:T(8,128)(2,1)S(1)} %copy-done), kind=kOutput, calls=%fused_computation.21 | convolution fusion | flops 8598323200 | bytes 34078720 | tf_op jit(solution)/shard_map/mi,mkd->ikd/dot_general | solution.py:30
  497.8 23.4 %copy.66 = bf16[512,64,256]{2,1,0:T(8,128)(2,1)} copy(bf16[512,64,256]{0,2,1:T(8,128)(2,1)} %convert_bitcast_fusion.2) | data formatting | bytes 33554432 | tf_op jit(solution)/shard_map/convert_element_type | solution.py:32
  521.2 5.7 all-to-all-start.1
  527.0 0.0 reduce-scatter.15.cloned.1.call-start
  527.0 1.0 copy.83
  528.0 0.0 reduce-scatter.15.cloned.1.call-update
  528.1 0.0 reduce-scatter.11.cloned.1.call-start
  528.1 35.8 %fusion.16 = f32[512,512]{1,0:T(8,128)} fusion(bf16[512,64,256]{0,2,1:T(8,128)(2,1)} %get-tuple-element.31, bf16[512,64,256]{2,1,0:T(8,128)(2,1)} %bitcast.68), kind=kOutput, calls=%fused_computation.29 | convolution fusion | flops 8589934592 | bytes 34603008 | tf_op jit(solution)/shard_map/mkd,ikd->mi/dot_general | solution.py:25
  563.9 23.3 %copy.73 = bf16[512,64,256]{2,1,0:T(8,128)(2,1)} copy(bf16[512,64,256]{0,2,1:T(8,128)(2,1)} %get-tuple-element.32) | data formatting | bytes 33554432
  587.2 0.0 reduce-scatter.11.cloned.1.call-update
  587.2 0.0 reduce-scatter.13.cloned.1.call-start
  587.3 308.1 %all-to-all-done.1 = bf16[512,64,256]{2,1,0:T(8,128)(2,1)} async-done(((bf16[512,64,256]{2,1,0:T(8,128)(2,1)}), bf16[512,64,256]{2,1,0:T(8,128)(2,1)}, u32[]{:S(2)}, u32[]{:S(2)}) %all-to-all-start.1) | async-done | bytes 16777248 | tf_op jit(solution)/shard_map/all_to_all | solution.py:33
  895.4 9.7 convert_bitcast_fusion
  905.1 11.1 copy.67
  916.2 33.4 %copy.68 = f32[64,512,256]{1,2,0:T(8,128)} copy(f32[64,512,256]{2,1,0:T(8,128)} %bitcast.66) | data formatting | bytes 67108864 | tf_op jit(solution)/shard_map/convert_element_type | solution.py:34
  949.6 0.0 copy-start.3
  949.6 16.8 %fusion.9 = f32[512,256]{0,1:T(8,128)S(1)} fusion(f32[64,512,256]{1,2,0:T(8,128)} %copy.68, bf16[64,256,512]{2,1,0:T(8,128)(2,1)} %get-tuple-element.34), kind=kLoop, calls=%fused_computation.17 | loop fusion | flops 25034752 | bytes 50855936 | tf_op jit(solution)/shard_map/reduce_sum | solution.py:35
  966.4 1.0 copy.81
  967.5 0.0 reduce-scatter.13.cloned.1.call-update
  967.5 0.0 copy-start.4
  967.5 0.0 reduce-scatter.9.cloned.1.call-start
  967.5 0.0 copy-done.3
  967.6 19.9 %fusion.15 = f32[512,512]{1,0:T(8,128)} fusion(bf16[64,512,256]{2,1,0:T(8,128)(2,1)} %param.6, f32[64,512,256]{1,2,0:T(8,128)} %copy.68, f32[512,256]{0,1:T(8,128)S(1)} %copy-done.3), kind=kOutput, calls=%fused_computation.28 | convolution fusion | flops 8606711808 | bytes 51904512 | tf_op jit(solution)/shard_map/ikd,ijd->kj/dot_general | solution.py:41
  987.4 0.0 reduce-scatter.9.cloned.1.call-update
  987.5 0.0 copy-done.4
  987.5 0.0 copy-start.1
  987.5 21.2 %convert_bitcast_fusion.1 = bf16[64,512,256]{1,2,0:T(8,128)(2,1)} fusion(f32[64,512,256]{1,2,0:T(8,128)} %copy.68, f32[512,256]{0,1:T(8,128)S(1)} %copy-done.3, bf16[512,512]{1,0:T(8,128)(2,1)S(1)} %copy-done.4), kind=kOutput, calls=%fused_computation.20 | convolution fusion | flops 8615100416 | bytes 51380224 | tf_op jit(solution)/shard_map/kj,ikd->ijd/dot_general | solution.py:37
  1008.6 22.4 %copy.74 = bf16[64,512,256]{2,1,0:T(8,128)(2,1)} copy(bf16[64,512,256]{1,2,0:T(8,128)(2,1)} %convert_bitcast_fusion.1) | data formatting | bytes 33554432
  1031.0 0.0 reduce-scatter.15.cloned.1.call-done
  1031.0 1.1 reduce-scatter.11.cloned.1.call-done
  1032.1 61.9 %reduce-scatter.13.cloned.1.call-done = f32[64,256]{1,0:T(8,128)} async-done(((f32[512,256]{1,0:T(8,128)}), f32[64,256]{1,0:T(8,128)}) %reduce-scatter.13.cloned.1.call-update) | async-done | bytes 65552
  1094.0 136.5 %reduce-scatter.9.cloned.1.call-done = f32[16,512]{1,0:T(8,128)} async-done(((f32[512,512]{1,0:T(8,128)}), f32[16,512]{1,0:T(8,128)}) %reduce-scatter.9.cloned.1.call-update) | async-done | bytes 32784 | tf_op jit(solution)/shard_map/reduce_scatter | solution.py:40
  1230.6 0.0 copy-done.1
Async XLA Ops:
  7.2 432.6 %copy-start = (bf16[512,512]{1,0:T(8,128)(2,1)S(1)}, bf16[512,512]{1,0:T(8,128)(2,1)}, u32[]{:S(2)}) copy-start(bf16[512,512]{1,0:T(8,128)(2,1)} %param.9) | copy-start | bytes 1572868
  8.3 19.8 %copy-start.2 = (f32[512,256]{0,1:T(8,128)}, f32[512,256]{0,1:T(8,128)S(1)}, u32[]{:S(2)}) copy-start(f32[512,256]{0,1:T(8,128)S(1)} %copy.59) | copy-start | bytes 1572868
  51.4 7.7 copy-start.5
  51.4 370.6 %all-to-all-start = ((bf16[64,512,256]{2,0,1:T(8,128)(2,1)}), bf16[64,512,256]{2,0,1:T(8,128)(2,1)}, u32[]{:S(2)}, u32[]{:S(2)}) async-start(bf16[64,512,256]{2,0,1:T(8,128)(2,1)} %copy.60), calls=%async_computation | async-start | bytes 33554432 | tf_op jit(solution)/shard_map/all_to_all | solution.py:13
  521.2 374.2 %all-to-all-start.1 = ((bf16[512,64,256]{2,1,0:T(8,128)(2,1)}), bf16[512,64,256]{2,1,0:T(8,128)(2,1)}, u32[]{:S(2)}, u32[]{:S(2)}) async-start(bf16[512,64,256]{2,1,0:T(8,128)(2,1)} %copy.66), calls=%async_computation.1 | async-start | bytes 33554432 | tf_op jit(solution)/shard_map/all_to_all | solution.py:33
  527.0 504.0 %reduce-scatter.15.cloned.1.call-start = ((), (), s32[]{:S(2)}) async-start(), calls=%async_computation.9 | async-start | bytes 589824
  528.1 504.1 %reduce-scatter.11.cloned.1.call-start = ((), (), s32[]{:S(2)}) async-start(), calls=%async_computation.7 | async-start | bytes 1081344 | tf_op jit(solution)/shard_map/reduce_scatter | solution.py:24
  587.2 506.8 %reduce-scatter.13.cloned.1.call-start = ((), (), s32[]{:S(2)}) async-start(), calls=%async_computation.8 | async-start | bytes 589824
  949.6 17.9 %copy-start.3 = (f32[512,256]{0,1:T(8,128)S(1)}, f32[512,256]{0,1:T(8,128)}, u32[]{:S(2)}) copy-start(f32[512,256]{0,1:T(8,128)} %copy-done.2) | copy-start | bytes 1572868
  967.5 20.0 %copy-start.4 = (bf16[512,512]{1,0:T(8,128)(2,1)S(1)}, bf16[512,512]{1,0:T(8,128)(2,1)}, u32[]{:S(2)}) copy-start(bf16[512,512]{1,0:T(8,128)(2,1)} %param.8) | copy-start | bytes 1572868
  967.5 263.1 %reduce-scatter.9.cloned.1.call-start = ((), (), s32[]{:S(2)}) async-start(), calls=%async_computation.6 | async-start | bytes 1081344 | tf_op jit(solution)/shard_map/reduce_scatter | solution.py:40
  987.5 243.1 %copy-start.1 = (bf16[512,512]{1,0:T(8,128)(2,1)S(1)}, bf16[512,512]{1,0:T(8,128)(2,1)}, u32[]{:S(2)}) copy-start(bf16[512,512]{1,0:T(8,128)(2,1)} %param.9) | copy-start | bytes 1572868
Sparse Core Ops, SparseCore 0:
  531.7 348.0 reduce-scatter.14
  882.8 149.3 reduce-scatter.10
  1036.1 57.9 reduce-scatter.12
  1096.8 133.7 reduce-scatter.8
where the time goes:
time: 1250 us; the launch traced here: 1240 us
  waiting for transfers between devices  846 us (68%)
  local copies, waits for them, and re-layouts  183 us (15%)
  matrix products  155 us (12%)
  other arithmetic  26.5 us (2%)
  between operations  14.1 us (1%)
  starting transfers between devices  13.6 us (1%)
    all_to_all x1, waiting for transfers between devices, per_device(): lax.all_to_all(panels, 'seq', split_axis=1, concat_axis=0, tiled=True)  338 us
    all_to_all x1, waiting for transfers between devices, per_device(): lax.all_to_all(grad_panels, 'seq', split_axis=0, concat_axis=1, tiled=True)  308 us
    reduce_scatter x1, waiting for transfers between devices, per_device(): lax.psum_scatter(jnp.einsum('ikd,ijd->kj', grad_section, inputs, preferre...  137 us
    unnamed x17, local copies, waits for them, and re-layouts  72.4 us
    unnamed x6, waiting for transfers between devices  62 us
    convert_element_type x2, local copies, waits for them, and re-layouts, per_device(): returned32 = returned.astype(jnp.float32)  44.5 us
    dot_general x1, matrix products, per_device(): jnp.einsum('mi,ikd->mkd', left_weight, received, preferred_element_type=j...  39.4 us
    dot_general x1, matrix products, per_device(): jnp.einsum('mkd,ikd->mi', grad_mixed, received, preferred_element_type=jn...  35.8 us
  transfers between devices with their start and end apart: 6, of which 5 were waited for; matrix products, arithmetic and copies ran while one was open for 18% of the time, Pallas kernels for 0%

commit v1 on v0

v1 whole, which is shorter than its diff:
```python
import functools

import jax
import jax.numpy as jnp
from jax import lax
from jax.experimental import pallas as pl
from jax.experimental.pallas import tpu as pltpu
from jax.sharding import PartitionSpec as P

BF16 = jnp.bfloat16
F32 = jnp.float32
LANES = 128
VMEM_LIMIT = 60 * 1024 * 1024


def section_kernel(blocks, w_ref, x_ref, out_ref):
    rows = x_ref.shape[0]
    w = w_ref[...]
    for first in range(0, rows, 2):
        pair = [x_ref[i] for i in range(first, min(first + 2, rows))]
        y = jnp.dot(w, jnp.concatenate(pair, axis=1), preferred_element_type=F32).astype(BF16)
        for p in range(len(pair)):
            part = y[:, p * LANES : (p + 1) * LANES]
            out_ref[:, first + p] = part.reshape(blocks, part.shape[0] // blocks, LANES)


def section_one(right, x, half, n):
    rows, cols, _ = x.shape
    step = min(8, rows)
    return pl.pallas_call(
        functools.partial(section_kernel, n),
        grid=(rows // step,),
        in_specs=[
            pl.BlockSpec((cols, cols), lambda i: (0, 0)),
            pl.BlockSpec((step, cols, LANES), lambda i: (i, 0, half)),
        ],
        out_specs=pl.BlockSpec((n, step, cols // n, LANES), lambda i: (0, i, 0, 0)),
        out_shape=jax.ShapeDtypeStruct((n, rows, cols // n, LANES), BF16),
        compiler_params=pltpu.CompilerParams(vmem_limit_bytes=VMEM_LIMIT),
        cost_estimate=pl.CostEstimate(
            flops=2 * rows * cols * cols * LANES,
            bytes_accessed=4 * rows * cols * LANES,
            transcendentals=0,
        ),
        name="section_one",
    )(right, x)


def joined(g_ref, i):
    block = g_ref[:, i]
    return block.reshape(block.shape[0] * block.shape[1], LANES)


def right_kernel(g_ref, x_ref, start_ref, out_ref, total):
    @pl.when(pl.program_id(0) == 0)
    def _():
        total[...] = start_ref[...]

    rows = x_ref.shape[0]
    g = jnp.concatenate([joined(g_ref, i) for i in range(rows)], axis=1)
    x = jnp.concatenate([x_ref[i] for i in range(rows)], axis=1)
    total[...] += lax.dot_general(g, x, (((1,), (1,)), ((), ())), preferred_element_type=F32)

    @pl.when(pl.program_id(0) == pl.num_programs(0) - 1)
    def _():
        out_ref[...] = total[...].astype(out_ref.dtype)


def grad_right_terms(g, x, half, start, dtype):
    n, rows, share, _ = g.shape
    cols = n * share
    step = min(8, rows)
    return pl.pallas_call(
        right_kernel,
        grid=(rows // step,),
        in_specs=[
            pl.BlockSpec((n, step, share, LANES), lambda i: (0, i, 0, 0)),
            pl.BlockSpec((step, cols, LANES), lambda i: (i, 0, half)),
            pl.BlockSpec((cols, cols), lambda i: (0, 0)),
        ],
        out_specs=pl.BlockSpec((cols, cols), lambda i: (0, 0)),
        out_shape=jax.ShapeDtypeStruct((cols, cols), dtype),
        scratch_shapes=[pltpu.VMEM((cols, cols), F32)],
        compiler_params=pltpu.CompilerParams(vmem_limit_bytes=VMEM_LIMIT),
        cost_estimate=pl.CostEstimate(
            flops=2 * rows * cols * cols * LANES,
            bytes_accessed=4 * rows * cols * LANES,
            transcendentals=0,
        ),
        name="grad_right",
    )(g, x, start)


def inputs_kernel(w_ref, g_ref, *refs):
    out_ref = refs[-1]
    rows = out_ref.shape[0]
    w = w_ref[...]
    for first in range(0, rows, 2):
        pair = [joined(g_ref, i) for i in range(first, min(first + 2, rows))]
        y = jnp.dot(w, jnp.concatenate(pair, axis=1), preferred_element_type=F32).astype(BF16)
        for p in range(len(pair)):
            out_ref[first + p] = y[:, p * LANES : (p + 1) * LANES]


def grad_inputs_half(right_t, g, half, channels, before):
    n, rows, share, _ = g.shape
    cols = n * share
    step = min(8, rows)
    in_specs = [
        pl.BlockSpec((cols, cols), lambda i: (0, 0)),
        pl.BlockSpec((n, step, share, LANES), lambda i: (0, i, 0, 0)),
    ]
    operands = [right_t, g]
    aliases = {}
    if before is not None:
        in_specs.append(pl.BlockSpec(memory_space=pl.ANY))
        operands.append(before)
        aliases = {2: 0}
    return pl.pallas_call(
        inputs_kernel,
        grid=(rows // step,),
        in_specs=in_specs,
        out_specs=pl.BlockSpec((step, cols, LANES), lambda i: (i, 0, half)),
        out_shape=jax.ShapeDtypeStruct((rows, cols, channels), BF16),
        input_output_aliases=aliases,
        compiler_params=pltpu.CompilerParams(vmem_limit_bytes=VMEM_LIMIT),
        cost_estimate=pl.CostEstimate(
            flops=2 * rows * cols * cols * LANES,
            bytes_accessed=4 * rows * cols * LANES,
            transcendentals=0,
        ),
        name="grad_inputs",
    )(*operands)


def place_kernel(part_ref, *refs):
    refs[-1][...] = part_ref[...]


def place_half(part, half, channels, before):
    rows, share, _ = part.shape
    step = min(64, rows)
    in_specs = [pl.BlockSpec((step, share, LANES), lambda i: (i, 0, 0))]
    operands = [part]
    aliases = {}
    if before is not None:
        in_specs.append(pl.BlockSpec(memory_space=pl.ANY))
        operands.append(before)
        aliases = {1: 0}
    return pl.pallas_call(
        place_kernel,
        grid=(rows // step,),
        in_specs=in_specs,
        out_specs=pl.BlockSpec((step, share, LANES), lambda i: (i, 0, half)),
        out_shape=jax.ShapeDtypeStruct((rows, share, channels), part.dtype),
        input_output_aliases=aliases,
        compiler_params=pltpu.CompilerParams(vmem_limit_bytes=VMEM_LIMIT),
        cost_estimate=pl.CostEstimate(
            flops=0, bytes_accessed=4 * rows * share * LANES, transcendentals=0
        ),
        name="place",
    )(*operands)


def scatter_sum(blocks, axis, size):
    if size & (size - 1):
        return lax.psum_scatter(blocks, axis, scatter_dimension=0)
    index = lax.axis_index(axis)
    bit = 1
    while bit < size:
        pairs = blocks.reshape((blocks.shape[0] // 2, 2) + blocks.shape[1:])
        mine = (index // bit) % 2
        kept = lax.dynamic_index_in_dim(pairs, mine, axis=1, keepdims=False)
        sent = lax.dynamic_index_in_dim(pairs, 1 - mine, axis=1, keepdims=False)
        blocks = kept + lax.ppermute(sent, axis, [(s, s ^ bit) for s in range(size)])
        bit *= 2
    return blocks[0]


def exchange(blocks):
    return lax.all_to_all(blocks, "seq", split_axis=0, concat_axis=0, tiled=True)


def middle(received, cotangent, left, gate_one, gate_two):
    n, rows, share, lanes = received.shape
    section = received.reshape(n * rows, share, lanes).astype(F32)
    gate_one = gate_one.astype(F32)[None]
    panels = (section * gate_one).astype(BF16)
    mixed = jnp.einsum("mi,ikd->mkd", left, panels, preferred_element_type=F32)
    logistic = jax.nn.sigmoid(mixed)
    activated = mixed * logistic
    gate_two = gate_two.astype(F32)[:, None, :]
    output = (activated * gate_two).astype(BF16)
    grad_out = cotangent.astype(F32)
    second = jnp.sum(grad_out * activated, axis=1)
    grad_mixed = (grad_out * gate_two * logistic * (1.0 + mixed * (1.0 - logistic))).astype(BF16)
    grad_left = jnp.einsum("mkd,ikd->mi", grad_mixed, panels, preferred_element_type=F32)
    grad_panels = jnp.einsum("mi,mkd->ikd", left, grad_mixed, preferred_element_type=F32)
    grad_panels = grad_panels.astype(BF16).astype(F32)
    first = jnp.sum(grad_panels * section, axis=0)
    grad_section = (grad_panels * gate_one).astype(BF16)
    return output, second, grad_left, first, grad_section.reshape(n, rows, share, lanes)


def per_device(sizes, inputs, cotangent, right_weight, left_weight, first_gate, second_gate):
    n, m = sizes
    rows, cols, channels = inputs.shape
    share = cols // n
    halves = channels // LANES
    mine = lax.dynamic_slice_in_dim(first_gate, lax.axis_index("seq") * share, share, axis=0)

    received = [exchange(section_one(right_weight, inputs, h, n)) for h in range(halves)]
    outs, seconds, lefts, firsts, returned = [], [], [], [], []
    for h in range(halves):
        lanes = slice(h * LANES, (h + 1) * LANES)
        output, second, left, first, grad_section = lax.optimization_barrier(
            middle(
                received[h],
                cotangent[:, :, lanes],
                left_weight,
                mine[:, lanes],
                second_gate[:, lanes],
            )
        )
        outs.append(output)
        seconds.append(second)
        lefts.append(left)
        firsts.append(first)
        returned.append(exchange(grad_section))

    grad_left = functools.reduce(jnp.add, lefts).reshape(n, m, -1, left_weight.shape[1])
    grad_left = scatter_sum(grad_left.swapaxes(0, 1), "ch", m)
    grad_second = jnp.concatenate(seconds, axis=1)
    both = jnp.concatenate([grad_left.reshape(n, -1), grad_second.reshape(n, -1)], axis=1)
    both = scatter_sum(both, "seq", n)
    size = grad_left.size // n
    grad_left = both[:size].reshape(-1, left_weight.shape[1])
    grad_second = both[size:].reshape(-1, channels)

    right_t = right_weight.T
    grad_first = jnp.concatenate(firsts, axis=1)
    output = None
    for h in range(halves):
        output = place_half(outs[h], h, channels, output)
    terms = jnp.zeros((cols, cols), F32)
    grad_inputs = None
    for h in range(halves - 1):
        terms = grad_right_terms(returned[h], inputs, h, terms, F32)
        grad_inputs = grad_inputs_half(right_t, returned[h], h, channels, grad_inputs)
    h = halves - 1
    returned[h], output, grad_first, terms, grad_inputs, right_t, grad_left, grad_second = (
        lax.optimization_barrier(
            (returned[h], output, grad_first, terms, grad_inputs, right_t, grad_left, grad_second)
        )
    )
    terms = grad_right_terms(returned[h], inputs, h, terms, BF16)
    terms = lax.all_to_all(
        terms.reshape(n * m, -1, cols), ("seq", "ch"), split_axis=0, concat_axis=0, tiled=True
    )
    grad_right = jnp.sum(terms.astype(F32), axis=0)
    grad_inputs = grad_inputs_half(right_t, returned[h], h, channels, grad_inputs)
    return output, grad_inputs, grad_right, grad_left, grad_first, grad_second


def solution(mesh):
    placed = (P("seq", None, "ch"), P(None, "seq", "ch"), P(), P(), P(None, "ch"), P(None, "ch"))
    return jax.shard_map(
        functools.partial(per_device, (mesh.shape["seq"], mesh.shape["ch"])),
        mesh=mesh,
        in_specs=placed,
        out_specs=(
            P(None, "seq", "ch"),
            P("seq", None, "ch"),
            P(("seq", "ch"), None),
            P(("seq", "ch"), None),
            P("seq", "ch"),
            P("seq", "ch"),
        ),
        check_vma=False,
    )
```

time: 1250 us -> 1040 us (0.83)
  waiting for transfers between devices: 846 us -> 641 us
  Pallas kernels: 0 us -> 85.5 us
  matrix products: 155 us -> 75.1 us
  local copies, waits for them, and re-layouts: 183 us -> 124 us
  other arithmetic: 26.5 us -> 62.5 us
  starting transfers between devices: 13.6 us -> 32.6 us
  between operations: 14.1 us -> 1.43 us
    all_to_all x2 -> x5, waiting for transfers between devices: 646 us -> 405 us  [the longest x4 400 us: exchange(): lax.all_to_all(blocks, 'seq', split_axis=0, concat_axis=0, tiled=True)]
    ppermute x0 -> x5, waiting for transfers between devices: none -> 236 us  [scatter_sum(): lax.ppermute(sent, axis, [(s, s ^ bit) for s in range(size)])]
    reduce_scatter x2 -> x0, waiting for transfers between devices: 138 us -> none  [the longest x1 137 us: per_device(): lax.psum_scatter(jnp.einsum('ikd,ijd->kj', grad_section, inputs, preferre...]
    pallas_call x0 -> x8, Pallas kernels: none -> 85.5 us  [the longest x2 23.5 us: grad_right_terms(): pl.pallas_call(right_kernel, grid=(rows // step,), in_specs=[pl.BlockSpec...]
    dot_general x6, matrix products: 155 us -> 75.1 us  [the longest x2 25.8 us: middle(): jnp.einsum('mi,mkd->ikd', left, grad_mixed, preferred_element_type=F32)]
    unnamed x17 -> x11, local copies, waits for them, and re-layouts: 72.4 us -> 1.51 us
    unnamed x6 -> x0, waiting for transfers between devices: 62 us -> none
    dot_general x0 -> x2, local copies, waits for them, and re-layouts: none -> 33.1 us  [middle(): mixed = jnp.einsum('mi,ikd->mkd', left, panels, preferred_element_type=F32)]
  transfers between devices with their start and end apart: 6 -> 10, of which waited for: 5 -> 7; matrix products, arithmetic and copies ran while one was open for 18% -> 7% of each run, Pallas kernels for 0% -> 6%
where the time goes in v1:
time: 1040 us; the launch traced here: 1020 us
  waiting for transfers between devices  641 us (62%)
  local copies, waits for them, and re-layouts  124 us (12%)
  Pallas kernels  85.5 us (8%)
  matrix products  75.1 us (7%)
  other arithmetic  62.5 us (6%)
  starting transfers between devices  32.6 us (3%)
    all_to_all x4, waiting for transfers between devices, exchange(): lax.all_to_all(blocks, 'seq', split_axis=0, concat_axis=0, tiled=True)  400 us
    ppermute x5, waiting for transfers between devices, scatter_sum(): lax.ppermute(sent, axis, [(s, s ^ bit) for s in range(size)])  236 us
    reduce_sum x1, other arithmetic, middle(): second = jnp.sum(grad_out * activated, axis=1)  35.1 us
    convert_element_type x2, local copies, waits for them, and re-layouts, middle(): section = received.reshape(n * rows, share, lanes).astype(F32)  34.9 us
    dot_general x2, local copies, waits for them, and re-layouts, middle(): mixed = jnp.einsum('mi,ikd->mkd', left, panels, preferred_element_type=F32)  33.1 us
    dot_general x2, matrix products, middle(): jnp.einsum('mi,mkd->ikd', left, grad_mixed, preferred_element_type=F32)  25.8 us
    convert_element_type x2, local copies, waits for them, and re-layouts, middle(): (grad_out * gate_two * logistic * (1.0 + mixed * (1.0 - logistic))).astyp...  25.8 us
    dot_general x2, matrix products, middle(): jnp.einsum('mkd,ikd->mi', grad_mixed, panels, preferred_element_type=F32)  25.4 us
  transfers between devices with their start and end apart: 10, of which 7 were waited for; matrix products, arithmetic and copies ran while one was open for 7% of the time, Pallas kernels for 6%

profile of v1, /device:TPU:0, one launch (start us, length us, event | category | flops | bytes accessed | tf_op | source)
XLA Modules:
  0.0 1022.5 jit_solution(13821632499575400057)
XLA Ops:
  0.6 11.0 %section_one.2 = bf16[8,64,64,128]{3,2,1,0:T(8,128)(2,1)} custom-call(bf16[512,512]{1,0:T(8,128)(2,1)} %w_ref.3, bf16[64,512,256]{2,1,0:T(8,128)(2,1)} %x_ref.7), custom_call_target="tpu_custom_call" | custom-call | flops 4294967296 | bytes 16777216 | tf_op jit(solution)/shard_map/section_one/pallas_call | solution.py:30
  11.7 7.3 all-to-all-start
  19.0 11.0 %section_one.3 = bf16[8,64,64,128]{3,2,1,0:T(8,128)(2,1)} custom-call(bf16[512,512]{1,0:T(8,128)(2,1)} %w_ref.3, bf16[64,512,256]{2,1,0:T(8,128)(2,1)} %x_ref.7), custom_call_target="tpu_custom_call" | custom-call | flops 4294967296 | bytes 16777216 | tf_op jit(solution)/shard_map/section_one/pallas_call | solution.py:30
  30.0 172.1 %all-to-all-done = bf16[8,64,64,128]{3,2,1,0:T(8,128)(2,1)} async-done(((bf16[8,64,64,128]{3,2,1,0:T(8,128)(2,1)}), bf16[8,64,64,128]{3,2,1,0:T(8,128)(2,1)}, u32[]{:S(2)}, u32[]{:S(2)}) %all-to-all-start) | async-done | bytes 8388640 | tf_op jit(solution)/shard_map/all_to_all | solution.py:181
  202.1 4.9 all-to-all-start.2
  207.1 0.7 dynamic-slice_convert_fusion
  207.9 11.7 %bitcast_convert_fusion.1 = f32[512,64,128]{2,1,0:T(8,128)} fusion(bf16[8,64,64,128]{3,2,1,0:T(8,128)(2,1)} %all-to-all-done), kind=kLoop, calls=%fused_computation.39 | loop fusion | flops 4194304 | bytes 25165824 | tf_op jit(solution)/shard_map/convert_element_type | solution.py:186
  219.6 17.5 %copy.44 = f32[512,64,128]{0,2,1:T(8,128)} copy(f32[512,64,128]{2,1,0:T(8,128)} %bitcast_convert_fusion.1) | data formatting | bytes 33554432 | tf_op jit(solution)/shard_map/convert_element_type | solution.py:186
  237.1 11.9 %fusion.21 = f32[64,128,512]{2,1,0:T(8,128)} fusion(f32[512,64,128]{0,2,1:T(8,128)} %copy.44, f32[64,128]{1,0:T(8,128)S(1)} %get-tuple-element.61, bf16[512,512]{1,0:T(8,128)(2,1)S(1)} %copy-done), kind=kOutput, calls=%fused_computation.43 | convolution fusion | flops 4303355904 | bytes 34111488 | tf_op jit(solution)/shard_map/mi,ikd->mkd/dot_general | solution.py:189
  249.1 16.5 %copy.45 = f32[64,128,512]{1,0,2:T(8,128)} copy(f32[64,128,512]{2,1,0:T(8,128)} %fusion.21) | data formatting | bytes 33554432 | tf_op jit(solution)/shard_map/mi,ikd->mkd/dot_general | solution.py:189
  265.6 123.7 %all-to-all-done.2 = bf16[8,64,64,128]{3,2,1,0:T(8,128)(2,1)} async-done(((bf16[8,64,64,128]{3,2,1,0:T(8,128)(2,1)}), bf16[8,64,64,128]{3,2,1,0:T(8,128)(2,1)}, u32[]{:S(2)}, u32[]{:S(2)}) %all-to-all-start.2) | async-done | bytes 8388640 | tf_op jit(solution)/shard_map/all_to_all | solution.py:181
  389.3 11.7 %bitcast_convert_fusion = f32[512,64,128]{2,1,0:T(8,128)} fusion(bf16[8,64,64,128]{3,2,1,0:T(8,128)(2,1)} %all-to-all-done.2), kind=kLoop, calls=%fused_computation.38 | loop fusion | flops 4194304 | bytes 25165824 | tf_op jit(solution)/shard_map/convert_element_type | solution.py:186
  401.0 17.5 %copy.51 = f32[512,64,128]{0,2,1:T(8,128)} copy(f32[512,64,128]{2,1,0:T(8,128)} %bitcast_convert_fusion) | data formatting | bytes 33554432 | tf_op jit(solution)/shard_map/convert_element_type | solution.py:186
  418.4 11.9 %fusion.23 = f32[64,128,512]{2,1,0:T(8,128)} fusion(f32[512,64,128]{0,2,1:T(8,128)} %copy.51, f32[64,128]{1,0:T(8,128)S(1)} %get-tuple-element.60, bf16[512,512]{1,0:T(8,128)(2,1)S(1)} %copy-done), kind=kOutput, calls=%fused_computation.45 | convolution fusion | flops 4303355904 | bytes 34111488 | tf_op jit(solution)/shard_map/mi,ikd->mkd/dot_general | solution.py:189
  430.4 16.5 %copy.52 = f32[64,128,512]{1,0,2:T(8,128)} copy(f32[64,128,512]{2,1,0:T(8,128)} %fusion.23) | data formatting | bytes 33554432 | tf_op jit(solution)/shard_map/mi,ikd->mkd/dot_general | solution.py:189
  446.9 35.1 %fusion.4 = (f32[512,128]{1,0:T(8,128)S(1)}, f32[512,128]{1,0:T(8,128)S(1)}, bf16[512,64,128]{2,1,0:T(8,128)(2,1)}, bf16[512,64,128]{2,1,0:T(8,128)(2,1)}, bf16[...) fusion(bf16[512,64,256]{2,1,0:T(8,128)(2,1)} %param.7, f32[64,128,512]{1,0,2:T(8,128)} %copy.52, ...), kind=kLoop, calls=%fused_computation.8 | loop fusion | flops 134086656 | bytes 84934656 | tf_op jit(solution)/shard_map/reduce_sum | solution.py:195
  482.0 12.9 %copy.55 = bf16[512,64,128]{0,2,1:T(8,128)(2,1)} copy(bf16[512,64,128]{2,1,0:T(8,128)(2,1)} %get-tuple-element.44) | data formatting | bytes 16777216 | tf_op jit(solution)/shard_map/convert_element_type | solution.py:196
  494.9 13.0 %fusion.9 = (bf16[512,64,128]{0,2,1:T(8,128)(2,1)}, f32[64,128]{1,0:T(8,128)S(1)}) fusion(f32[64,128]{1,0:T(8,128)S(1)} %get-tuple-element.60, f32[512,64,128]{0,2,1:T(8,128)} %copy.51, bf16[512,64,128]{0,2,1:T(8,128)(2,1)} %copy.55, bf16[512,512]{1,0:T(8,128)(2,1)S(1)} %copy-done), kind=kOutput, calls=%fused_computation.15 | convolution fusion | flops 4320124928 | bytes 34144256 | tf_op jit(solution)/shard_map/mi,mkd->ikd/dot_general | solution.py:198
  507.9 12.7 %fusion.24 = f32[512,512]{1,0:T(8,128)S(1)} fusion(bf16[512,64,128]{0,2,1:T(8,128)(2,1)} %copy.55, f32[512,64,128]{0,2,1:T(8,128)} %copy.51, f32[64,128]{1,0:T(8,128)S(1)} %get-tuple-element.60), kind=kOutput, calls=%fused_computation.46 | convolution fusion | flops 4303355904 | bytes 26247168 | tf_op jit(solution)/shard_map/mkd,ikd->mi/dot_general | solution.py:197
  520.6 12.8 %copy.48 = bf16[512,64,128]{0,2,1:T(8,128)(2,1)} copy(bf16[512,64,128]{2,1,0:T(8,128)(2,1)} %get-tuple-element.45) | data formatting | bytes 16777216 | tf_op jit(solution)/shard_map/convert_element_type | solution.py:196
  533.5 12.8 %fusion.15 = (bf16[512,64,128]{0,2,1:T(8,128)(2,1)}, f32[64,128]{1,0:T(8,128)S(1)}) fusion(f32[64,128]{1,0:T(8,128)S(1)} %get-tuple-element.61, f32[512,64,128]{0,2,1:T(8,128)} %copy.44, bf16[512,64,128]{0,2,1:T(8,128)(2,1)} %copy.48, bf16[512,512]{1,0:T(8,128)(2,1)S(1)} %copy-done), kind=kOutput, calls=%fused_computation.26 | convolution fusion | flops 4320124928 | bytes 34144256 | tf_op jit(solution)/shard_map/mi,mkd->ikd/dot_general | solution.py:198
  546.3 12.7 %fusion.25 = f32[512,512]{1,0:T(8,128)S(1)} fusion(bf16[512,64,128]{0,2,1:T(8,128)(2,1)} %copy.48, f32[512,64,128]{0,2,1:T(8,128)} %copy.44, f32[64,128]{1,0:T(8,128)S(1)} %get-tuple-element.61), kind=kOutput, calls=%fused_computation.47 | convolution fusion | flops 4303355904 | bytes 26247168 | tf_op jit(solution)/shard_map/mkd,ikd->mi/dot_general | solution.py:197
  559.0 11.9 %copy.57 = bf16[512,64,128]{2,1,0:T(8,128)(2,1)} copy(bf16[512,64,128]{0,2,1:T(8,128)(2,1)} %get-tuple-element.48) | data formatting | bytes 16777216 | tf_op jit(solution)/shard_map/convert_element_type | solution.py:201
  570.9 12.2 %copy.50 = bf16[512,64,128]{2,1,0:T(8,128)(2,1)} copy(bf16[512,64,128]{0,2,1:T(8,128)(2,1)} %get-tuple-element.50) | data formatting | bytes 16777216 | tf_op jit(solution)/shard_map/convert_element_type | solution.py:201
  583.1 0.2 add.99
  583.3 0.1 constant_dynamic-slice_fusion.7
  583.6 5.0 all-to-all-start.3
  588.6 0.1 fusion.26
  588.7 1.6 collective-permute-start.1
  590.4 0.3 concatenate.17
  590.7 6.9 collective-permute-done.1
  597.6 1.0 dynamic-slice_add_fusion
  598.6 0.2 concatenate.15
  598.9 0.7 constant_dynamic-slice_fusion.4
  599.6 0.3 copy.78
  599.9 1.7 collective-permute-start.2
  601.5 65.0 %collective-permute-done.2 = f32[4,24576]{1,0:T(4,128)S(1)} collective-permute-done((f32[4,24576]{1,0:T(4,128)S(1)}, f32[4,24576]{1,0:T(4,128)S(1)}, u32[]{:S(2)}, u32[]{:S(2)}) %collective-permute-start.2) | collective-permute-done | bytes 393248 | tf_op jit(solution)/shard_map/ppermute | solution.py:175
  666.5 0.3 bitcast_add_fusion
  666.8 0.3 reshape.70
  667.1 0.3 constant_dynamic-slice_fusion.2
  667.5 0.2 copy.79
  667.7 0.6 collective-permute-start.3
  668.3 104.3 %all-to-all-done.3.g_ref = bf16[8,64,64,128]{3,2,1,0:T(8,128)(2,1)} async-done(((bf16[8,64,64,128]{3,2,1,0:T(8,128)(2,1)}), bf16[8,64,64,128]{3,2,1,0:T(8,128)(2,1)}, u32[]{:S(2)}, u32[]{:S(2)}) %all-to-all-start.3) | async-done | bytes 8388640 | tf_op jit(solution)/shard_map/all_to_all | solution.py:181
  772.6 5.0 all-to-all-start.1
  777.6 1.0 copy.58
  778.7 8.9 place.2.refs_0_
  787.6 8.9 place.3
  796.6 0.2 bitcast_add_fusion.1
  796.8 0.1 constant_dynamic-slice_fusion
  796.9 2.8 collective-permute-start.4
  799.7 0.6 pad_maximum_fusion.1
  800.3 164.5 %collective-permute-done.4 = f32[1,24576]{1,0:T(1,128)S(1)} collective-permute-done((f32[1,24576]{1,0:T(1,128)S(1)}, f32[1,24576]{1,0:T(1,128)S(1)}, u32[]{:S(2)}, u32[]{:S(2)}) %collective-permute-start.4) | collective-permute-done | bytes 98336 | tf_op jit(solution)/shard_map/ppermute | solution.py:175
  964.9 0.1 dynamic-slice_add_fusion.1
  965.0 0.2 slice_reduce_fusion
  965.2 0.6 reshape.72
  965.9 0.6 reshape.71
  966.5 11.0 %grad_inputs.2.refs_0_ = bf16[64,512,256]{2,1,0:T(8,128)(2,1)} custom-call(bf16[512,512]{1,0:T(8,128)(2,1)} %bitcast.115, bf16[8,64,64,128]{3,2,1,0:T(8,128)(2,1)} %all-to-all-done.3.g_ref), custom_call_target="tpu_custom_call" | custom-call | flops 4294967296 | bytes 16777216 | tf_op jit(solution)/shard_map/grad_inputs/pallas_call | solution.py:119
  977.5 1.1 broadcast_in_dim.2.start_ref
  978.6 11.9 %grad_right.2.start_ref = f32[512,512]{1,0:T(8,128)} custom-call(bf16[8,64,64,128]{3,2,1,0:T(8,128)(2,1)} %all-to-all-done.3.g_ref, bf16[64,512,256]{2,1,0:T(8,128)(2,1)} %x_ref.7, f32[512,512]{1,0:T(8,128)} %broadcast_in_dim.2.start_ref), custom_call_target="tpu_custom_call" | custom-call | flops 4294967296 | bytes 16777216 | tf_op jit(solution)/shard_map/grad_right/pallas_call | solution.py:73
  990.5 11.6 %grad_right.3 = bf16[512,512]{1,0:T(8,128)(2,1)} custom-call(bf16[8,64,64,128]{3,2,1,0:T(8,128)(2,1)} %all-to-all-done.1.g_ref, bf16[64,512,256]{2,1,0:T(8,128)(2,1)} %x_ref.7, f32[512,512]{1,0:T(8,128)} %grad_right.2.start_ref), custom_call_target="tpu_custom_call" | custom-call | flops 4294967296 | bytes 16777216 | tf_op jit(solution)/shard_map/grad_right/pallas_call | solution.py:73
  1002.1 3.7 all-to-all-start.4
  1005.8 11.0 %grad_inputs.3 = bf16[64,512,256]{2,1,0:T(8,128)(2,1)} custom-call(bf16[512,512]{1,0:T(8,128)(2,1)} %bitcast.116, bf16[8,64,64,128]{3,2,1,0:T(8,128)(2,1)} %all-to-all-done.1.g_ref, bf16[64,512,256]{2,1,0:T(8,128)(2,1)} %grad_inputs.2.refs_0_), custom_call_target="tpu_custom_call", output_to_operand_aliasing={{}: (2, {})} | custom-call | flops 4294967296 | bytes 16777216 | tf_op jit(solution)/shard_map/grad_inputs/pallas_call | solution.py:119
  1016.8 4.5 all-to-all-done.4
  1021.3 0.7 convert_reduce_fusion
  (17 shorter events, 0.4 us)
Async XLA Ops:
  0.6 236.5 %copy-start = (bf16[512,512]{1,0:T(8,128)(2,1)S(1)}, bf16[512,512]{1,0:T(8,128)(2,1)}, u32[]{:S(2)}) copy-start(bf16[512,512]{1,0:T(8,128)(2,1)} %param.9) | copy-start | bytes 1572868
  11.7 190.5 %all-to-all-start = ((bf16[8,64,64,128]{3,2,1,0:T(8,128)(2,1)}), bf16[8,64,64,128]{3,2,1,0:T(8,128)(2,1)}, u32[]{:S(2)}, u32[]{:S(2)}) async-start(bf16[8,64,64,128]{3,2,1,0:T(8,128)(2,1)} %section_one.2), calls=%async_computation | async-start | bytes 16777216 | tf_op jit(solution)/shard_map/all_to_all | solution.py:181
  19.0 188.9 %copy-start.2 = (bf16[512,256]{1,0:T(8,128)(2,1)S(1)}, bf16[512,256]{1,0:T(8,128)(2,1)}, u32[]{:S(2)}) copy-start(bf16[512,256]{1,0:T(8,128)(2,1)} %param.11) | copy-start | bytes 786436
  202.1 187.1 %all-to-all-start.2 = ((bf16[8,64,64,128]{3,2,1,0:T(8,128)(2,1)}), bf16[8,64,64,128]{3,2,1,0:T(8,128)(2,1)}, u32[]{:S(2)}, u32[]{:S(2)}) async-start(bf16[8,64,64,128]{3,2,1,0:T(8,128)(2,1)} %section_one.3), calls=%async_computation.2 | async-start | bytes 16777216 | tf_op jit(solution)/shard_map/all_to_all | solution.py:181
  583.5 5.1 collective-permute-start
  583.6 189.0 %all-to-all-start.3 = ((bf16[8,64,64,128]{3,2,1,0:T(8,128)(2,1)}), bf16[8,64,64,128]{3,2,1,0:T(8,128)(2,1)}, u32[]{:S(2)}, u32[]{:S(2)}) async-start(bf16[8,64,64,128]{3,2,1,0:T(8,128)(2,1)} %bitcast.114), calls=%async_computation.3 | async-start | bytes 16777216 | tf_op jit(solution)/shard_map/all_to_all | solution.py:181
  588.6 189.0 %copy-start.1 = (bf16[512,512]{1,0:T(8,128)(2,1)S(1)}, bf16[512,512]{1,0:T(8,128)(2,1)}, u32[]{:S(2)}) copy-start(bf16[512,512]{1,0:T(8,128)(2,1)} %w_ref.3) | copy-start | bytes 1572868
  588.7 8.8 collective-permute-start.1
  599.9 66.7 %collective-permute-start.2 = (f32[4,24576]{1,0:T(4,128)S(1)}, f32[4,24576]{1,0:T(4,128)S(1)}, u32[]{:S(2)}, u32[]{:S(2)}) collective-permute-start(f32[4,24576]{1,0:T(4,128)S(1)} %bitcast.120), channel_id=1, source_target_pairs={{0,4},{4,0},{8,12},{12,8},{16,20},{20,16},{24,28},{28,24},{1,5},{5... | collective-permute-start | bytes 1179656 | tf_op jit(solution)/shard_map/ppermute | solution.py:175
  667.7 128.9 %collective-permute-start.3 = (f32[2,24576]{1,0:T(2,128)S(1)}, f32[2,24576]{1,0:T(2,128)S(1)}, u32[]{:S(2)}, u32[]{:S(2)}) collective-permute-start(f32[2,24576]{1,0:T(2,128)S(1)} %bitcast.121), channel_id=1, source_target_pairs={{0,8},{4,12},{8,0},{12,4},{16,24},{20,28},{24,16},{28,20},{1,9},{5... | collective-permute-start | bytes 589832 | tf_op jit(solution)/shard_map/ppermute | solution.py:175
  772.6 217.9 %all-to-all-start.1 = ((bf16[8,64,64,128]{3,2,1,0:T(8,128)(2,1)}), bf16[8,64,64,128]{3,2,1,0:T(8,128)(2,1)}, u32[]{:S(2)}, u32[]{:S(2)}) async-start(bf16[8,64,64,128]{3,2,1,0:T(8,128)(2,1)} %bitcast.113), calls=%async_computation.1 | async-start | bytes 16777216 | tf_op jit(solution)/shard_map/all_to_all | solution.py:181
  796.9 168.0 %collective-permute-start.4 = (f32[1,24576]{1,0:T(1,128)S(1)}, f32[1,24576]{1,0:T(1,128)S(1)}, u32[]{:S(2)}, u32[]{:S(2)}) collective-permute-start(f32[1,24576]{1,0:T(1,128)S(1)} %constant_dynamic-slice_fusion), channel_id=1, source_target_pairs={{0,16},{4,20},{8,24},{12,28},{16,0},{20,4},{24,8},{28,12},{1,17},{... | collective-permute-start | bytes 294920 | tf_op jit(solution)/shard_map/ppermute | solution.py:175
  1002.1 19.2 %all-to-all-start.4 = ((bf16[32,16,512]{2,1,0:T(8,128)(2,1)}), bf16[32,16,512]{2,1,0:T(8,128)(2,1)S(1)}, u32[]{:S(2)}, u32[]{:S(2)}) async-start(bf16[32,16,512]{2,1,0:T(8,128)(2,1)} %bitcast.118), calls=%async_computation.4 | async-start | bytes 1048576 | tf_op jit(solution)/shard_map/all_to_all | solution.py:257

commit v2 on v1

--- a/solution.py
+++ b/solution.py
@@ -133,73 +133,127 @@
     )(*operands)
 
 
-def place_kernel(part_ref, *refs):
-    refs[-1][...] = part_ref[...]
-
-
-def place_half(part, half, channels, before):
-    rows, share, _ = part.shape
-    step = min(64, rows)
-    in_specs = [pl.BlockSpec((step, share, LANES), lambda i: (i, 0, 0))]
-    operands = [part]
+def scatter_sum(blocks, axis, size, dtype):
+    if size & (size - 1):
+        return lax.psum_scatter(blocks, axis, scatter_dimension=0)
+    index = lax.axis_index(axis)
+    low = 1
+    while low < size:
+        radix = min(8, size // low)
+        groups = blocks.reshape((blocks.shape[0] // radix, radix) + blocks.shape[1:])
+        mine = (index // low) % radix
+        blocks = lax.dynamic_index_in_dim(groups, mine, axis=1, keepdims=False)
+        groups = groups.astype(dtype)
+        for d in range(1, radix):
+            sent = lax.dynamic_index_in_dim(groups, mine ^ d, axis=1, keepdims=False)
+            pairs = [(s, s ^ (d * low)) for s in range(size)]
+            blocks = blocks + lax.ppermute(sent, axis, pairs).astype(F32)
+        low *= radix
+    return blocks[0]
+
+
+def exchange(blocks):
+    return lax.all_to_all(blocks, "seq", split_axis=0, concat_axis=0, tiled=True)
+
+
+def middle_kernel(
+    left_ref, left_t_ref, s_ref, cot_ref, gate_one_ref, gate_two_ref, *refs
+):
+    out_ref, section_ref, terms_ref, first_ref, second_ref, terms, second = refs[-7:]
+    group = pl.program_id(0)
+    count = s_ref.shape[2]
+    size = s_ref.shape[0] * s_ref.shape[1]
+    part = min(8, count)
+
+    @pl.when(group == 0)
+    def _():
+        terms[...] = jnp.zeros_like(terms)
+        second[...] = jnp.zeros_like(second)
+
+    def wide(value):
+        return pltpu.einshape("akc->a(kc)", value)
+
+    def deep(value):
+        return pltpu.einshape("a(kc)->akc", value, k=part)
+
+    gate_two = jnp.concatenate([gate_two_ref[...].astype(F32)] * part, axis=1)
+    for k in range(0, count, part):
+        near = slice(k, k + part)
+        gate_one = gate_one_ref[near].astype(F32)
+        gate_one = jnp.concatenate([gate_one[j : j + 1] for j in range(part)], axis=1)
+        section = wide(s_ref[:, :, near].reshape(size, part, LANES)).astype(F32)
+        panels = (section * gate_one).astype(BF16)
+        mixed = jnp.dot(left_ref[...], panels, preferred_element_type=F32)
+        logistic = 1.0 / (1.0 + jnp.exp(-mixed))
+        activated = mixed * logistic
+        out_ref[:, near] = deep((activated * gate_two).astype(BF16))
+        cot = wide(cot_ref[:, near]).astype(F32)
+        gated = cot * activated
+        second[...] += sum(gated[:, j * LANES : (j + 1) * LANES] for j in range(part))
+        grad = cot * gate_two * logistic * (1.0 + mixed * (1.0 - logistic))
+        grad = grad.astype(BF16)
+        terms[...] += lax.dot_general(
+            grad, panels, (((1,), (1,)), ((), ())), preferred_element_type=F32
+        )
+        back = jnp.dot(left_t_ref[...], grad, preferred_element_type=F32).astype(BF16).astype(F32)
+        sums = jnp.sum(back * section, axis=0, keepdims=True)
+        for j in range(part):
+            first_ref[k + j : k + j + 1, :] = sums[:, j * LANES : (j + 1) * LANES]
+        back = deep((back * gate_one).astype(BF16))
+        section_ref[:, :, near] = back.reshape(s_ref.shape[0], s_ref.shape[1], part, LANES)
+
+    @pl.when(group == pl.num_programs(0) - 1)
+    def _():
+        terms_ref[...] = terms[...]
+        second_ref[...] = second[...]
+
+
+def middle(received, cotangent, left, left_t, gate_one, gate_two, half, before):
+    n, rows, share, _ = received.shape
+    size = n * rows
+    step = min(16, share)
+    in_specs = [
+        pl.BlockSpec((size, size), lambda i: (0, 0)),
+        pl.BlockSpec((size, size), lambda i: (0, 0)),
+        pl.BlockSpec((n, rows, step, LANES), lambda i: (0, 0, i, 0)),
+        pl.BlockSpec((size, step, LANES), lambda i: (0, i, half)),
+        pl.BlockSpec((step, LANES), lambda i: (i, half)),
+        pl.BlockSpec((size, LANES), lambda i: (0, half)),
+    ]
+    operands = [left, left_t, received, cotangent, gate_one, gate_two]
     aliases = {}
     if before is not None:
         in_specs.append(pl.BlockSpec(memory_space=pl.ANY))
+        aliases = {len(operands): 0}
         operands.append(before)
-        aliases = {1: 0}
     return pl.pallas_call(
-        place_kernel,
-        grid=(rows // step,),
+        middle_kernel,
+        grid=(share // step,),
         in_specs=in_specs,
-        out_specs=pl.BlockSpec((step, share, LANES), lambda i: (i, 0, half)),
-        out_shape=jax.ShapeDtypeStruct((rows, share, channels), part.dtype),
+        out_specs=[
+            pl.BlockSpec((size, step, LANES), lambda i: (0, i, half)),
+            pl.BlockSpec((n, rows, step, LANES), lambda i: (0, 0, i, 0)),
+            pl.BlockSpec((size, size), lambda i: (0, 0)),
+            pl.BlockSpec((step, LANES), lambda i: (i, 0)),
+            pl.BlockSpec((size, LANES), lambda i: (0, 0)),
+        ],
+        out_shape=[
+            jax.ShapeDtypeStruct(cotangent.shape, BF16),
+            jax.ShapeDtypeStruct(received.shape, BF16),
+            jax.ShapeDtypeStruct((size, size), F32),
+            jax.ShapeDtypeStruct((share, LANES), F32),
+            jax.ShapeDtypeStruct((size, LANES), F32),
+        ],
+        scratch_shapes=[pltpu.VMEM((size, size), F32), pltpu.VMEM((size, LANES), F32)],
         input_output_aliases=aliases,
         compiler_params=pltpu.CompilerParams(vmem_limit_bytes=VMEM_LIMIT),
         cost_estimate=pl.CostEstimate(
-            flops=0, bytes_accessed=4 * rows * share * LANES, transcendentals=0
-        ),
-        name="place",
+            flops=6 * size * size * share * LANES,
+            bytes_accessed=8 * size * share * LANES,
+            transcendentals=size * share * LANES,
+        ),
+        name="middle",
     )(*operands)
-
-
-def scatter_sum(blocks, axis, size):
-    if size & (size - 1):
-        return lax.psum_scatter(blocks, axis, scatter_dimension=0)
-    index = lax.axis_index(axis)
-    bit = 1
-    while bit < size:
-        pairs = blocks.reshape((blocks.shape[0] // 2, 2) + blocks.shape[1:])
-        mine = (index // bit) % 2
-        kept = lax.dynamic_index_in_dim(pairs, mine, axis=1, keepdims=False)
-        sent = lax.dynamic_index_in_dim(pairs, 1 - mine, axis=1, keepdims=False)
-        blocks = kept + lax.ppermute(sent, axis, [(s, s ^ bit) for s in range(size)])
-        bit *= 2
-    return blocks[0]
-
-
-def exchange(blocks):
-    return lax.all_to_all(blocks, "seq", split_axis=0, concat_axis=0, tiled=True)
-
-
-def middle(received, cotangent, left, gate_one, gate_two):
-    n, rows, share, lanes = received.shape
-    section = received.reshape(n * rows, share, lanes).astype(F32)
-    gate_one = gate_one.astype(F32)[None]
-    panels = (section * gate_one).astype(BF16)
-    mixed = jnp.einsum("mi,ikd->mkd", left, panels, preferred_element_type=F32)
-    logistic = jax.nn.sigmoid(mixed)
-    activated = mixed * logistic
-    gate_two = gate_two.astype(F32)[:, None, :]
-    output = (activated * gate_two).astype(BF16)
-    grad_out = cotangent.astype(F32)
-    second = jnp.sum(grad_out * activated, axis=1)
-    grad_mixed = (grad_out * gate_two * logistic * (1.0 + mixed * (1.0 - logistic))).astype(BF16)
-    grad_left = jnp.einsum("mkd,ikd->mi", grad_mixed, panels, preferred_element_type=F32)
-    grad_panels = jnp.einsum("mi,mkd->ikd", left, grad_mixed, preferred_element_type=F32)
-    grad_panels = grad_panels.astype(BF16).astype(F32)
-    first = jnp.sum(grad_panels * section, axis=0)
-    grad_section = (grad_panels * gate_one).astype(BF16)
-    return output, second, grad_left, first, grad_section.reshape(n, rows, share, lanes)
 
 
 def per_device(sizes, inputs, cotangent, right_weight, left_weight, first_gate, second_gate):
@@ -210,48 +264,37 @@
     mine = lax.dynamic_slice_in_dim(first_gate, lax.axis_index("seq") * share, share, axis=0)
 
     received = [exchange(section_one(right_weight, inputs, h, n)) for h in range(halves)]
-    outs, seconds, lefts, firsts, returned = [], [], [], [], []
+    left_t = left_weight.T
+    output = None
+    seconds, lefts, firsts, returned = [], [], [], []
     for h in range(halves):
-        lanes = slice(h * LANES, (h + 1) * LANES)
-        output, second, left, first, grad_section = lax.optimization_barrier(
-            middle(
-                received[h],
-                cotangent[:, :, lanes],
-                left_weight,
-                mine[:, lanes],
-                second_gate[:, lanes],
-            )
+        output, grad_section, left, first, second = middle(
+            received[h], cotangent, left_weight, left_t, mine, second_gate, h, output
         )
-        outs.append(output)
         seconds.append(second)
         lefts.append(left)
         firsts.append(first)
         returned.append(exchange(grad_section))
 
     grad_left = functools.reduce(jnp.add, lefts).reshape(n, m, -1, left_weight.shape[1])
-    grad_left = scatter_sum(grad_left.swapaxes(0, 1), "ch", m)
+    grad_left = scatter_sum(grad_left.swapaxes(0, 1), "ch", m, F32)
     grad_second = jnp.concatenate(seconds, axis=1)
     both = jnp.concatenate([grad_left.reshape(n, -1), grad_second.reshape(n, -1)], axis=1)
-    both = scatter_sum(both, "seq", n)
+    both = scatter_sum(both, "seq", n, BF16)
     size = grad_left.size // n
     grad_left = both[:size].reshape(-1, left_weight.shape[1])
     grad_second = both[size:].reshape(-1, channels)
 
     right_t = right_weight.T
     grad_first = jnp.concatenate(firsts, axis=1)
-    output = None
-    for h in range(halves):
-        output = place_half(outs[h], h, channels, output)
     terms = jnp.zeros((cols, cols), F32)
     grad_inputs = None
     for h in range(halves - 1):
         terms = grad_right_terms(returned[h], inputs, h, terms, F32)
         grad_inputs = grad_inputs_half(right_t, returned[h], h, channels, grad_inputs)
     h = halves - 1
-    returned[h], output, grad_first, terms, grad_inputs, right_t, grad_left, grad_second = (
-        lax.optimization_barrier(
-            (returned[h], output, grad_first, terms, grad_inputs, right_t, grad_left, grad_second)
-        )
+    returned[h], grad_first, terms, grad_inputs, right_t = lax.optimization_barrier(
+        (returned[h], grad_first, terms, grad_inputs, right_t)
     )
     terms = grad_right_terms(returned[h], inputs, h, terms, BF16)
     terms = lax.all_to_all(

time: 1040 us -> 806 us (0.78); the launches traced: 1020 us -> 805 us
  local copies, waits for them, and re-layouts: 124 us -> 7.6 us
  matrix products: 75.1 us -> 0 us
  other arithmetic: 62.5 us -> 3.12 us
  Pallas kernels: 85.5 us -> 134 us
  waiting for transfers between devices: 641 us -> 620 us
    ppermute x5 -> x10, waiting for transfers between devices: 236 us -> 10.2 us  [scatter_sum(): blocks = blocks + lax.ppermute(sent, axis, pairs).astype(F32)]
    all_to_all x4, waiting for transfers between devices: 400 us -> 607 us  [exchange(): lax.all_to_all(blocks, 'seq', split_axis=0, concat_axis=0, tiled=True)]
    convert_element_type x6 -> x0, local copies, waits for them, and re-layouts: 84.8 us -> none  [the longest x2 34.9 us: middle(): section = received.reshape(n * rows, share, lanes).astype(F32)]
    dot_general x6 -> x0, matrix products: 75.1 us -> none  [the longest x2 25.8 us: middle(): jnp.einsum('mi,mkd->ikd', left, grad_mixed, preferred_element_type=F32)]
    pallas_call x2, Pallas kernels: 17.9 us -> 66.6 us  [middle(): pl.pallas_call(middle_kernel, grid=(share // step,), in_specs=in_specs, o...]
    reduce_sum x1 -> x0, other arithmetic: 35.1 us -> none  [middle(): second = jnp.sum(grad_out * activated, axis=1)]
    dot_general x2 -> x0, local copies, waits for them, and re-layouts: 33.1 us -> none  [middle(): mixed = jnp.einsum('mi,ikd->mkd', left, panels, preferred_element_type=F32)]
    convert_element_type x4 -> x0, other arithmetic: 24.2 us -> none  [the longest x2 23.4 us: middle(): section = received.reshape(n * rows, share, lanes).astype(F32)]
  transfers between devices with their start and end apart: 10 -> 15, of which waited for: 7 -> 7; matrix products, arithmetic and copies ran while one was open for 7% -> 1% of each run, Pallas kernels for 6% -> 15%
where the time goes in v2:
time: 806 us; the launch traced here: 805 us
  waiting for transfers between devices  620 us (77%)
  Pallas kernels  134 us (17%)
  starting transfers between devices  38.9 us (5%)
    all_to_all x4, waiting for transfers between devices, exchange(): lax.all_to_all(blocks, 'seq', split_axis=0, concat_axis=0, tiled=True)  607 us
    pallas_call x2, Pallas kernels, middle(): pl.pallas_call(middle_kernel, grid=(share // step,), in_specs=in_specs, o...  66.6 us
    pallas_call x2, Pallas kernels, grad_right_terms(): pl.pallas_call(right_kernel, grid=(rows // step,), in_specs=[pl.BlockSpec...  23.5 us
    all_to_all x4, starting transfers between devices, exchange(): lax.all_to_all(blocks, 'seq', split_axis=0, concat_axis=0, tiled=True)  22.9 us
    pallas_call x2, Pallas kernels, grad_inputs_half(): pl.pallas_call(inputs_kernel, grid=(rows // step,), in_specs=in_specs, ou...  22 us
    pallas_call x2, Pallas kernels, section_one(): pl.pallas_call(functools.partial(section_kernel, n), grid=(rows // step,)...  22 us
  transfers between devices with their start and end apart: 15, of which 7 were waited for; matrix products, arithmetic and copies ran while one was open for 1% of the time, Pallas kernels for 15%

profile of v2, /device:TPU:0, one launch (start us, length us, event | category | flops | bytes accessed | tf_op | source)
XLA Modules:
  0.0 804.8 jit_solution(5201944328279553694)
XLA Ops:
  0.6 0.0 copy-start
  0.6 11.0 %section_one.3 = bf16[8,64,64,128]{3,2,1,0:T(8,128)(2,1)} custom-call(bf16[512,512]{1,0:T(8,128)(2,1)} %w_ref.3, bf16[64,512,256]{2,1,0:T(8,128)(2,1)} %x_ref.7), custom_call_target="tpu_custom_call" | custom-call | flops 4294967296 | bytes 16777216 | tf_op jit(solution)/shard_map/section_one/pallas_call | solution.py:30
  11.7 7.3 all-to-all-start.1
  19.0 11.0 %section_one.2 = bf16[8,64,64,128]{3,2,1,0:T(8,128)(2,1)} custom-call(bf16[512,512]{1,0:T(8,128)(2,1)} %w_ref.3, bf16[64,512,256]{2,1,0:T(8,128)(2,1)} %x_ref.7), custom_call_target="tpu_custom_call" | custom-call | flops 4294967296 | bytes 16777216 | tf_op jit(solution)/shard_map/section_one/pallas_call | solution.py:30
  30.0 172.2 %all-to-all-done.1.s_ref = bf16[8,64,64,128]{3,2,1,0:T(8,128)(2,1)} async-done(((bf16[8,64,64,128]{3,2,1,0:T(8,128)(2,1)}), bf16[8,64,64,128]{3,2,1,0:T(8,128)(2,1)}, u32[]{:S(2)}, u32[]{:S(2)}) %all-to-all-start.1) | async-done | bytes 8388640 | tf_op jit(solution)/shard_map/all_to_all | solution.py:156
  202.1 5.0 all-to-all-start
  207.1 1.0 copy.16
  208.1 0.0 copy-done
  208.2 0.6 constant_dynamic-slice_fusion.gate_one_ref
  208.8 33.2 %middle.2 = (bf16[512,64,256]{2,1,0:T(8,128)(2,1)}, bf16[8,64,64,128]{3,2,1,0:T(8,128)(2,1)}, f32[512,512]{1,0:T(8,128)}, f32[64,128]{1,0:T(8,128)}, f32[512,128]{1,0:T(8,128)}) custom-call(bf16[512,512]{1,0:T(8,128)(2,1)} %left_ref.3, bf16[512,512]{1,0:T(8,128)(2,1)} %bitcast.50, bf16[8,64,64,128]{3,2,1,0:T(8,128)(2,1)} %all-to-all-done.1.s_ref, ...), custom_call_target="tpu_custom_call" | custom-call | flops 12884901888 | bytes 33554432 | tf_op jit(solution)/shard_map/middle/pallas_call | solution.py:229
  242.0 147.3 %all-to-all-done.s_ref = bf16[8,64,64,128]{3,2,1,0:T(8,128)(2,1)} async-done(((bf16[8,64,64,128]{3,2,1,0:T(8,128)(2,1)}), bf16[8,64,64,128]{3,2,1,0:T(8,128)(2,1)}, u32[]{:S(2)}, u32[]{:S(2)}) %all-to-all-start) | async-done | bytes 8388640 | tf_op jit(solution)/shard_map/all_to_all | solution.py:156
  389.3 5.2 all-to-all-start.3
  394.5 33.3 %middle.3 = (bf16[512,64,256]{2,1,0:T(8,128)(2,1)}, bf16[8,64,64,128]{3,2,1,0:T(8,128)(2,1)}, f32[512,512]{1,0:T(8,128)}, f32[64,128]{1,0:T(8,128)}, f32[512,128]{1,0:T(8,128)}) custom-call(bf16[512,512]{1,0:T(8,128)(2,1)} %left_ref.3, bf16[512,512]{1,0:T(8,128)(2,1)} %bitcast.51, ...), custom_call_target="tpu_custom_call", output_to_operand_aliasing={{0}: (6, {})} | custom-call | flops 12884901888 | bytes 33554432 | tf_op jit(solution)/shard_map/middle/pallas_call | solution.py:229
  427.8 148.5 %all-to-all-done.3.g_ref = bf16[8,64,64,128]{3,2,1,0:T(8,128)(2,1)} async-done(((bf16[8,64,64,128]{3,2,1,0:T(8,128)(2,1)}), bf16[8,64,64,128]{3,2,1,0:T(8,128)(2,1)}, u32[]{:S(2)}, u32[]{:S(2)}) %all-to-all-start.3) | async-done | bytes 8388640 | tf_op jit(solution)/shard_map/all_to_all | solution.py:156
  576.3 5.5 all-to-all-start.2
  581.8 0.0 copy-start.7
  581.8 0.0 copy-start.8
  581.9 1.0 copy.17
  582.9 0.0 copy-done.3
  582.9 0.2 add.85
  583.1 0.1 dynamic-slice_bitcast_fusion.2
  583.2 0.1 collective-permute-start
  583.3 1.6 collective-permute-start.1
  584.8 0.3 collective-permute-start.2
  585.2 1.0 constant_dynamic-update-slice_fusion
  586.2 0.1 reshape.83
  586.3 0.1 concatenate.27
  586.4 0.0 copy-done.7
  586.4 0.6 pad_maximum_fusion
  587.1 0.0 collective-permute-done
  587.1 5.5 collective-permute-done.1
  592.6 4.7 collective-permute-done.2
  597.3 1.1 fusion.4
  598.4 0.1 concatenate.26
  598.5 0.7 dynamic-slice_bitcast_fusion.9
  599.2 1.6 collective-permute-start.3
  600.9 1.5 collective-permute-start.4
  602.4 0.4 collective-permute-start.5
  602.8 2.5 collective-permute-start.6
  605.3 1.4 collective-permute-start.7
  606.7 0.2 copy.26
  606.9 11.0 %grad_inputs.2.refs_0_ = bf16[64,512,256]{2,1,0:T(8,128)(2,1)} custom-call(bf16[512,512]{1,0:T(8,128)(2,1)} %bitcast.44, bf16[8,64,64,128]{3,2,1,0:T(8,128)(2,1)} %all-to-all-done.3.g_ref), custom_call_target="tpu_custom_call" | custom-call | flops 4294967296 | bytes 16777216 | tf_op jit(solution)/shard_map/grad_inputs/pallas_call | solution.py:119
  617.9 1.1 broadcast_in_dim.3.start_ref
  619.0 11.9 %grad_right.2.start_ref = f32[512,512]{1,0:T(8,128)} custom-call(bf16[8,64,64,128]{3,2,1,0:T(8,128)(2,1)} %all-to-all-done.3.g_ref, bf16[64,512,256]{2,1,0:T(8,128)(2,1)} %x_ref.7, f32[512,512]{1,0:T(8,128)} %broadcast_in_dim.3.start_ref), custom_call_target="tpu_custom_call" | custom-call | flops 4294967296 | bytes 16777216 | tf_op jit(solution)/shard_map/grad_right/pallas_call | solution.py:73
  630.9 139.4 %all-to-all-done.2.g_ref = bf16[8,64,64,128]{3,2,1,0:T(8,128)(2,1)} async-done(((bf16[8,64,64,128]{3,2,1,0:T(8,128)(2,1)}), bf16[8,64,64,128]{3,2,1,0:T(8,128)(2,1)}, u32[]{:S(2)}, u32[]{:S(2)}) %all-to-all-start.2) | async-done | bytes 8388640 | tf_op jit(solution)/shard_map/all_to_all | solution.py:156
  770.4 0.0 collective-permute-done.3
  770.4 0.6 collective-permute-start.8
  770.9 0.0 collective-permute-done.4
  770.9 3.3 collective-permute-start.9
  774.3 11.6 %grad_right.3 = bf16[512,512]{1,0:T(8,128)(2,1)} custom-call(bf16[8,64,64,128]{3,2,1,0:T(8,128)(2,1)} %all-to-all-done.2.g_ref, bf16[64,512,256]{2,1,0:T(8,128)(2,1)} %x_ref.7, f32[512,512]{1,0:T(8,128)} %grad_right.2.start_ref), custom_call_target="tpu_custom_call" | custom-call | flops 4294967296 | bytes 16777216 | tf_op jit(solution)/shard_map/grad_right/pallas_call | solution.py:73
  785.9 2.7 all-to-all-start.4
  788.6 0.0 collective-permute-done.5
  788.6 0.0 collective-permute-done.6
  788.6 0.0 collective-permute-done.7
  788.6 0.0 collective-permute-done.8
  788.6 0.0 collective-permute-done.9
  788.6 0.4 convert_add_fusion
  789.1 0.2 slice_reduce_fusion
  789.3 0.6 reshape.85
  789.9 0.1 slice_reduce_fusion.1
  790.0 0.6 reshape.84
  790.6 11.0 %grad_inputs.3 = bf16[64,512,256]{2,1,0:T(8,128)(2,1)} custom-call(bf16[512,512]{1,0:T(8,128)(2,1)} %bitcast.45, bf16[8,64,64,128]{3,2,1,0:T(8,128)(2,1)} %all-to-all-done.2.g_ref, bf16[64,512,256]{2,1,0:T(8,128)(2,1)} %grad_inputs.2.refs_0_), custom_call_target="tpu_custom_call", output_to_operand_aliasing={{}: (2, {})} | custom-call | flops 4294967296 | bytes 16777216 | tf_op jit(solution)/shard_map/grad_inputs/pallas_call | solution.py:119
  801.7 2.5 all-to-all-done.4
  804.1 0.7 convert_reduce_fusion
  (16 shorter events, 0.1 us)
Async XLA Ops:
  0.6 207.5 %copy-start = (bf16[512,256]{1,0:T(8,128)(2,1)S(1)}, bf16[512,256]{1,0:T(8,128)(2,1)}, u32[]{:S(2)}) copy-start(bf16[512,256]{1,0:T(8,128)(2,1)} %param.10) | copy-start | bytes 786436
  11.7 190.4 %all-to-all-start.1 = ((bf16[8,64,64,128]{3,2,1,0:T(8,128)(2,1)}), bf16[8,64,64,128]{3,2,1,0:T(8,128)(2,1)}, u32[]{:S(2)}, u32[]{:S(2)}) async-start(bf16[8,64,64,128]{3,2,1,0:T(8,128)(2,1)} %section_one.3), calls=%async_computation.1 | async-start | bytes 16777216 | tf_op jit(solution)/shard_map/all_to_all | solution.py:156
  30.0 177.2 %copy-start.5 = (bf16[512,512]{1,0:T(8,128)(2,1)S(1)}, bf16[512,512]{1,0:T(8,128)(2,1)}, u32[]{:S(2)}) copy-start(bf16[512,512]{1,0:T(8,128)(2,1)} %left_ref.3) | copy-start | bytes 1572868
  202.1 187.2 %all-to-all-start = ((bf16[8,64,64,128]{3,2,1,0:T(8,128)(2,1)}), bf16[8,64,64,128]{3,2,1,0:T(8,128)(2,1)}, u32[]{:S(2)}, u32[]{:S(2)}) async-start(bf16[8,64,64,128]{3,2,1,0:T(8,128)(2,1)} %section_one.2), calls=%async_computation | async-start | bytes 16777216 | tf_op jit(solution)/shard_map/all_to_all | solution.py:156
  389.3 187.0 %all-to-all-start.3 = ((bf16[8,64,64,128]{3,2,1,0:T(8,128)(2,1)}), bf16[8,64,64,128]{3,2,1,0:T(8,128)(2,1)}, u32[]{:S(2)}, u32[]{:S(2)}) async-start(bf16[8,64,64,128]{3,2,1,0:T(8,128)(2,1)} %get-tuple-element.26), calls=%async_computation.3 | async-start | bytes 16777216 | tf_op jit(solution)/shard_map/all_to_all | solution.py:156
  576.3 5.6 copy-start.2
  576.3 6.6 copy-start.3
  576.3 6.6 copy-start.4
  576.3 8.8 %copy-start.6 = (f32[512,128]{1,0:T(8,128)S(1)}, f32[512,128]{1,0:T(8,128)}, u32[]{:S(2)}) copy-start(f32[512,128]{1,0:T(8,128)} %get-tuple-element.33) | copy-start | bytes 786436
  576.3 194.1 %all-to-all-start.2 = ((bf16[8,64,64,128]{3,2,1,0:T(8,128)(2,1)}), bf16[8,64,64,128]{3,2,1,0:T(8,128)(2,1)}, u32[]{:S(2)}, u32[]{:S(2)}) async-start(bf16[8,64,64,128]{3,2,1,0:T(8,128)(2,1)} %get-tuple-element.23), calls=%async_computation.2 | async-start | bytes 16777216 | tf_op jit(solution)/shard_map/all_to_all | solution.py:156
  581.8 4.6 copy-start.7
  581.8 4.6 copy-start.8
  583.2 3.9 collective-permute-start
  583.3 9.3 %collective-permute-start.1 = (f32[1,8,16,512]{3,2,1,0:T(8,128)S(1)}, f32[1,8,16,512]{3,2,1,0:T(8,128)}, u32[]{:S(2)}, u32[]{:S(2)}) collective-permute-start(f32[1,8,16,512]{3,2,1,0:T(8,128)S(1)} %get-tuple-element.39), channel_id=1, source_target_pairs={{0,2},{1,3},{2,0},{3,1},{4,6},{5,7},{6,4},{7,5},{8,10},{9,11},{10,... | collective-permute-start | bytes 786440 | tf_op jit(solution)/shard_map/ppermute | solution.py:150
  584.8 12.4 %collective-permute-start.2 = (f32[1,8,16,512]{3,2,1,0:T(8,128)S(1)}, f32[1,8,16,512]{3,2,1,0:T(8,128)}, u32[]{:S(2)}, u32[]{:S(2)}) collective-permute-start(f32[1,8,16,512]{3,2,1,0:T(8,128)S(1)} %get-tuple-element.40), channel_id=1, source_target_pairs={{0,3},{1,2},{2,1},{3,0},{4,7},{5,6},{6,5},{7,4},{8,11},{9,10},{10,... | collective-permute-start | bytes 786440 | tf_op jit(solution)/shard_map/ppermute | solution.py:150
  599.2 171.1 %collective-permute-start.3 = (bf16[1,24576]{1,0:T(2,128)(2,1)S(1)}, bf16[1,24576]{1,0:T(2,128)(2,1)S(1)}, u32[]{:S(2)}, u32[]{:S(2)}) collective-permute-start(bf16[1,24576]{1,0:T(2,128)(2,1)S(1)} %get-tuple-element.41), channel_id=1, source_target_pairs={{0,4},{4,0},{8,12},{12,8},{16,20},{20,16},{24,28},{28,24},{1,5},{5... | collective-permute-start | bytes 147464 | tf_op jit(solution)/shard_map/ppermute | solution.py:150
  600.9 170.1 %collective-permute-start.4 = (bf16[1,24576]{1,0:T(2,128)(2,1)S(1)}, bf16[1,24576]{1,0:T(2,128)(2,1)S(1)}, u32[]{:S(2)}, u32[]{:S(2)}) collective-permute-start(bf16[1,24576]{1,0:T(2,128)(2,1)S(1)} %get-tuple-element.47), channel_id=1, source_target_pairs={{0,8},{4,12},{8,0},{12,4},{16,24},{20,28},{24,16},{28,20},{1,9},{5... | collective-permute-start | bytes 147464 | tf_op jit(solution)/shard_map/ppermute | solution.py:150
  602.4 186.2 %collective-permute-start.5 = (bf16[1,24576]{1,0:T(2,128)(2,1)S(1)}, bf16[1,24576]{1,0:T(2,128)(2,1)S(1)}, u32[]{:S(2)}, u32[]{:S(2)}) collective-permute-start(bf16[1,24576]{1,0:T(2,128)(2,1)S(1)} %get-tuple-element.46), channel_id=1, source_target_pairs={{0,12},{4,8},{8,4},{12,0},{16,28},{20,24},{24,20},{28,16},{1,13},{... | collective-permute-start | bytes 147464 | tf_op jit(solution)/shard_map/ppermute | solution.py:150
  602.8 185.8 %collective-permute-start.6 = (bf16[1,24576]{1,0:T(2,128)(2,1)S(1)}, bf16[1,24576]{1,0:T(2,128)(2,1)S(1)}, u32[]{:S(2)}, u32[]{:S(2)}) collective-permute-start(bf16[1,24576]{1,0:T(2,128)(2,1)S(1)} %get-tuple-element.45), channel_id=1, source_target_pairs={{0,16},{4,20},{8,24},{12,28},{16,0},{20,4},{24,8},{28,12},{1,17},{... | collective-permute-start | bytes 147464 | tf_op jit(solution)/shard_map/ppermute | solution.py:150
  605.3 183.3 %collective-permute-start.7 = (bf16[1,24576]{1,0:T(2,128)(2,1)S(1)}, bf16[1,24576]{1,0:T(2,128)(2,1)S(1)}, u32[]{:S(2)}, u32[]{:S(2)}) collective-permute-start(bf16[1,24576]{1,0:T(2,128)(2,1)S(1)} %get-tuple-element.44), channel_id=1, source_target_pairs={{0,20},{4,16},{8,28},{12,24},{16,4},{20,0},{24,12},{28,8},{1,21},{... | collective-permute-start | bytes 147464 | tf_op jit(solution)/shard_map/ppermute | solution.py:150
  770.4 18.2 %collective-permute-start.8 = (bf16[1,24576]{1,0:T(2,128)(2,1)S(1)}, bf16[1,24576]{1,0:T(2,128)(2,1)S(1)}, u32[]{:S(2)}, u32[]{:S(2)}) collective-permute-start(bf16[1,24576]{1,0:T(2,128)(2,1)S(1)} %get-tuple-element.43), channel_id=1, source_target_pairs={{0,24},{4,28},{8,16},{12,20},{16,8},{20,12},{24,0},{28,4},{1,25},{... | collective-permute-start | bytes 147464 | tf_op jit(solution)/shard_map/ppermute | solution.py:150
  770.9 17.7 %collective-permute-start.9 = (bf16[1,24576]{1,0:T(2,128)(2,1)S(1)}, bf16[1,24576]{1,0:T(2,128)(2,1)S(1)}, u32[]{:S(2)}, u32[]{:S(2)}) collective-permute-start(bf16[1,24576]{1,0:T(2,128)(2,1)S(1)} %get-tuple-element.42), channel_id=1, source_target_pairs={{0,28},{4,24},{8,20},{12,16},{16,12},{20,8},{24,4},{28,0},{1,29},{... | collective-permute-start | bytes 147464 | tf_op jit(solution)/shard_map/ppermute | solution.py:150
  785.9 18.3 %all-to-all-start.4 = ((bf16[32,16,512]{2,1,0:T(8,128)(2,1)}), bf16[32,16,512]{2,1,0:T(8,128)(2,1)S(1)}, u32[]{:S(2)}, u32[]{:S(2)}) async-start(bf16[32,16,512]{2,1,0:T(8,128)(2,1)} %bitcast.48), calls=%async_computation.4 | async-start | bytes 1048576 | tf_op jit(solution)/shard_map/all_to_all | solution.py:300
  790.6 14.2 %copy-start.1 = (bf16[512,256]{1,0:T(8,128)(2,1)S(1)}, bf16[512,256]{1,0:T(8,128)(2,1)}, u32[]{:S(2)}) copy-start(bf16[512,256]{1,0:T(8,128)(2,1)} %param.10) | copy-start | bytes 786436

commit v3 on v2

--- a/solution.py
+++ b/solution.py
@@ -13,29 +13,50 @@
 VMEM_LIMIT = 60 * 1024 * 1024
 
 
-def section_kernel(blocks, w_ref, x_ref, out_ref):
-    rows = x_ref.shape[0]
-    w = w_ref[...]
-    for first in range(0, rows, 2):
-        pair = [x_ref[i] for i in range(first, min(first + 2, rows))]
-        y = jnp.dot(w, jnp.concatenate(pair, axis=1), preferred_element_type=F32).astype(BF16)
-        for p in range(len(pair)):
-            part = y[:, p * LANES : (p + 1) * LANES]
-            out_ref[:, first + p] = part.reshape(blocks, part.shape[0] // blocks, LANES)
+def section_kernel(half, step, w_ref, x_ref, out_ref, x_buf, out_buf, in_sems, out_sems):
+    blocks, rows, share, _ = out_buf.shape
+
+    def fetch(c):
+        near = pl.ds(c * step, step)
+        lanes = pl.ds(half * LANES, LANES)
+        return pltpu.make_async_copy(x_ref.at[near, :, lanes], x_buf.at[near], in_sems.at[c])
+
+    def store(c):
+        near = pl.ds(c * step, step)
+        return pltpu.make_async_copy(out_buf.at[:, near], out_ref.at[:, near], out_sems.at[c])
+
+    for c in range(rows // step):
+        fetch(c).start()
+    for c in range(rows // step):
+        fetch(c).wait()
+        group = jnp.concatenate([x_buf[c * step + i] for i in range(step)], axis=1)
+        y = jnp.dot(w_ref[...], group, preferred_element_type=F32).astype(BF16)
+        for i in range(step):
+            part = y[:, i * LANES : (i + 1) * LANES]
+            out_buf[:, c * step + i] = part.reshape(blocks, share, LANES)
+        store(c).start()
+    for c in range(rows // step):
+        store(c).wait()
 
 
 def section_one(right, x, half, n):
     rows, cols, _ = x.shape
     step = min(8, rows)
+    count = rows // step
     return pl.pallas_call(
-        functools.partial(section_kernel, n),
-        grid=(rows // step,),
+        functools.partial(section_kernel, half, step),
         in_specs=[
-            pl.BlockSpec((cols, cols), lambda i: (0, 0)),
-            pl.BlockSpec((step, cols, LANES), lambda i: (i, 0, half)),
-        ],
-        out_specs=pl.BlockSpec((n, step, cols // n, LANES), lambda i: (0, i, 0, 0)),
+            pl.BlockSpec(memory_space=pltpu.VMEM),
+            pl.BlockSpec(memory_space=pl.ANY),
+        ],
+        out_specs=pl.BlockSpec(memory_space=pl.ANY),
         out_shape=jax.ShapeDtypeStruct((n, rows, cols // n, LANES), BF16),
+        scratch_shapes=[
+            pltpu.VMEM((rows, cols, LANES), BF16),
+            pltpu.VMEM((n, rows, cols // n, LANES), BF16),
+            pltpu.SemaphoreType.DMA((count,)),
+            pltpu.SemaphoreType.DMA((count,)),
+        ],
         compiler_params=pltpu.CompilerParams(vmem_limit_bytes=VMEM_LIMIT),
         cost_estimate=pl.CostEstimate(
             flops=2 * rows * cols * cols * LANES,
@@ -51,36 +72,54 @@
     return block.reshape(block.shape[0] * block.shape[1], LANES)
 
 
-def right_kernel(g_ref, x_ref, start_ref, out_ref, total):
-    @pl.when(pl.program_id(0) == 0)
-    def _():
-        total[...] = start_ref[...]
-
-    rows = x_ref.shape[0]
-    g = jnp.concatenate([joined(g_ref, i) for i in range(rows)], axis=1)
-    x = jnp.concatenate([x_ref[i] for i in range(rows)], axis=1)
-    total[...] += lax.dot_general(g, x, (((1,), (1,)), ((), ())), preferred_element_type=F32)
-
-    @pl.when(pl.program_id(0) == pl.num_programs(0) - 1)
-    def _():
-        out_ref[...] = total[...].astype(out_ref.dtype)
+def right_kernel(
+    half, step, g_ref, x_ref, start_ref, out_ref, g_buf, x_buf, total, g_sems, x_sems
+):
+    rows = x_buf.shape[0]
+
+    def fetch(c):
+        near = pl.ds(c * step, step)
+        lanes = pl.ds(half * LANES, LANES)
+        return (
+            pltpu.make_async_copy(g_ref.at[:, near], g_buf.at[:, near], g_sems.at[c]),
+            pltpu.make_async_copy(x_ref.at[near, :, lanes], x_buf.at[near], x_sems.at[c]),
+        )
+
+    for c in range(rows // step):
+        for copy in fetch(c):
+            copy.start()
+    total[...] = start_ref[...]
+    for c in range(rows // step):
+        for copy in fetch(c):
+            copy.wait()
+        near = range(c * step, (c + 1) * step)
+        g = jnp.concatenate([joined(g_buf, i) for i in near], axis=1)
+        x = jnp.concatenate([x_buf[i] for i in near], axis=1)
+        total[...] += lax.dot_general(g, x, (((1,), (1,)), ((), ())), preferred_element_type=F32)
+    out_ref[...] = total[...].astype(out_ref.dtype)
 
 
 def grad_right_terms(g, x, half, start, dtype):
     n, rows, share, _ = g.shape
     cols = n * share
     step = min(8, rows)
+    count = rows // step
     return pl.pallas_call(
-        right_kernel,
-        grid=(rows // step,),
+        functools.partial(right_kernel, half, step),
         in_specs=[
-            pl.BlockSpec((n, step, share, LANES), lambda i: (0, i, 0, 0)),
-            pl.BlockSpec((step, cols, LANES), lambda i: (i, 0, half)),
-            pl.BlockSpec((cols, cols), lambda i: (0, 0)),
-        ],
-        out_specs=pl.BlockSpec((cols, cols), lambda i: (0, 0)),
+            pl.BlockSpec(memory_space=pl.ANY),
+            pl.BlockSpec(memory_space=pl.ANY),
+            pl.BlockSpec(memory_space=pltpu.VMEM),
+        ],
+        out_specs=pl.BlockSpec(memory_space=pltpu.VMEM),
         out_shape=jax.ShapeDtypeStruct((cols, cols), dtype),
-        scratch_shapes=[pltpu.VMEM((cols, cols), F32)],
+        scratch_shapes=[
+            pltpu.VMEM((n, rows, share, LANES), BF16),
+            pltpu.VMEM((rows, cols, LANES), BF16),
+            pltpu.VMEM((cols, cols), F32),
+            pltpu.SemaphoreType.DMA((count,)),
+            pltpu.SemaphoreType.DMA((count,)),
+        ],
         compiler_params=pltpu.CompilerParams(vmem_limit_bytes=VMEM_LIMIT),
         cost_estimate=pl.CostEstimate(
             flops=2 * rows * cols * cols * LANES,
@@ -152,8 +191,10 @@
     return blocks[0]
 
 
-def exchange(blocks):
-    return lax.all_to_all(blocks, "seq", split_axis=0, concat_axis=0, tiled=True)
+def exchange(blocks, groups=None):
+    return lax.all_to_all(
+        blocks, "seq", split_axis=0, concat_axis=0, tiled=True, axis_index_groups=groups
+    )
 
 
 def middle_kernel(
@@ -278,12 +319,19 @@
 
     grad_left = functools.reduce(jnp.add, lefts).reshape(n, m, -1, left_weight.shape[1])
     grad_left = scatter_sum(grad_left.swapaxes(0, 1), "ch", m, F32)
+    size = grad_left.size // n
     grad_second = jnp.concatenate(seconds, axis=1)
     both = jnp.concatenate([grad_left.reshape(n, -1), grad_second.reshape(n, -1)], axis=1)
-    both = scatter_sum(both, "seq", n, BF16)
-    size = grad_left.size // n
-    grad_left = both[:size].reshape(-1, left_weight.shape[1])
-    grad_second = both[size:].reshape(-1, channels)
+    if n % 2 == 0:
+        me = lax.axis_index("seq") % 2
+        pairs = both.reshape(n // 2, 2, -1)
+        sent = lax.dynamic_index_in_dim(pairs, 1 - me, axis=1, keepdims=False).astype(BF16)
+        both = lax.dynamic_index_in_dim(pairs, me, axis=1, keepdims=False)
+        both = both + lax.ppermute(sent, "seq", [(s, s ^ 1) for s in range(n)]).astype(F32)
+        groups = [list(range(b, n, 2)) for b in range(2)]
+    else:
+        groups = None
+    both = both.astype(BF16).reshape(both.shape[0], -1, LANES)
 
     right_t = right_weight.T
     grad_first = jnp.concatenate(firsts, axis=1)
@@ -293,9 +341,13 @@
         terms = grad_right_terms(returned[h], inputs, h, terms, F32)
         grad_inputs = grad_inputs_half(right_t, returned[h], h, channels, grad_inputs)
     h = halves - 1
-    returned[h], grad_first, terms, grad_inputs, right_t = lax.optimization_barrier(
-        (returned[h], grad_first, terms, grad_inputs, right_t)
+    returned[h], both, grad_first, terms, grad_inputs, right_t = lax.optimization_barrier(
+        (returned[h], both, grad_first, terms, grad_inputs, right_t)
     )
+    both = exchange(both, groups)
+    both = jnp.sum(both.astype(F32), axis=0).reshape(-1)
+    grad_left = both[:size].reshape(-1, left_weight.shape[1])
+    grad_second = both[size:].reshape(-1, channels)
     terms = grad_right_terms(returned[h], inputs, h, terms, BF16)
     terms = lax.all_to_all(
         terms.reshape(n * m, -1, cols), ("seq", "ch"), split_axis=0, concat_axis=0, tiled=True

time: 806 us -> 798 us (0.990)
  Pallas kernels: 134 us -> 125 us
    ppermute x0 -> x1, waiting for transfers between devices: none -> 50.7 us  [per_device(): lax.ppermute(sent, 'seq', [(s, s ^ 1) for s in range(n)]).astype(F32)]
    all_to_all x4 -> x5, waiting for transfers between devices: 607 us -> 557 us  [exchange(): lax.all_to_all(blocks, 'seq', split_axis=0, concat_axis=0, tiled=True, ax...]
    ppermute x10 -> x3, starting transfers between devices: 13.3 us -> 1.86 us  [scatter_sum(): blocks = blocks + lax.ppermute(sent, axis, pairs).astype(F32)]
    pallas_call x4, Pallas kernels: 45.6 us -> 36.2 us  [the longest x2 18.2 us: section_one(): pl.pallas_call(functools.partial(section_kernel, half, step), in_specs=[p...]
    all_to_all x4 -> x5, starting transfers between devices: 22.9 us -> 27.1 us  [exchange(): lax.all_to_all(blocks, 'seq', split_axis=0, concat_axis=0, tiled=True, ax...]
  transfers between devices with their start and end apart: 15 -> 10, of which waited for: 7 -> 8; matrix products, arithmetic and copies ran while one was open for 1% -> 2% of each run, Pallas kernels for 15% -> 15%
where the time goes in v3:
time: 798 us; the launch traced here: 797 us
  waiting for transfers between devices  622 us (78%)
  Pallas kernels  125 us (16%)
  starting transfers between devices  35.9 us (4%)
    all_to_all x5, waiting for transfers between devices, exchange(): lax.all_to_all(blocks, 'seq', split_axis=0, concat_axis=0, tiled=True, ax...  557 us
    pallas_call x2, Pallas kernels, middle(): pl.pallas_call(middle_kernel, grid=(share // step,), in_specs=in_specs, o...  66.5 us
    ppermute x1, waiting for transfers between devices, per_device(): lax.ppermute(sent, 'seq', [(s, s ^ 1) for s in range(n)]).astype(F32)  50.7 us
    all_to_all x5, starting transfers between devices, exchange(): lax.all_to_all(blocks, 'seq', split_axis=0, concat_axis=0, tiled=True, ax...  27.1 us
    pallas_call x2, Pallas kernels, grad_inputs_half(): pl.pallas_call(inputs_kernel, grid=(rows // step,), in_specs=in_specs, ou...  22 us
    pallas_call x2, Pallas kernels, section_one(): pl.pallas_call(functools.partial(section_kernel, half, step), in_specs=[p...  18.2 us
    pallas_call x2, Pallas kernels, grad_right_terms(): pl.pallas_call(functools.partial(right_kernel, half, step), in_specs=[pl....  17.9 us
  transfers between devices with their start and end apart: 10, of which 8 were waited for; matrix products, arithmetic and copies ran while one was open for 2% of the time, Pallas kernels for 15%

profile of v3, /device:TPU:0, one launch (start us, length us, event | category | flops | bytes accessed | tf_op | source)
XLA Modules:
  0.0 796.5 jit_solution(6998890115661857854)
XLA Ops:
  0.6 0.0 copy-start
  0.6 9.1 %section_one.3 = bf16[8,64,64,128]{3,2,1,0:T(8,128)(2,1)} custom-call(bf16[512,512]{1,0:T(8,128)(2,1)} %w_ref.3, bf16[64,512,256]{2,1,0:T(8,128)(2,1)} %x_ref.7), custom_call_target="tpu_custom_call" | custom-call | flops 4294967296 | bytes 16777216 | tf_op jit(solution)/shard_map/section_one/pallas_call | solution.py:46
  9.8 7.3 all-to-all-start.1
  17.1 9.1 %section_one.2 = bf16[8,64,64,128]{3,2,1,0:T(8,128)(2,1)} custom-call(bf16[512,512]{1,0:T(8,128)(2,1)} %w_ref.3, bf16[64,512,256]{2,1,0:T(8,128)(2,1)} %x_ref.7), custom_call_target="tpu_custom_call" | custom-call | flops 4294967296 | bytes 16777216 | tf_op jit(solution)/shard_map/section_one/pallas_call | solution.py:46
  26.2 0.0 copy-start.4
  26.2 174.0 %all-to-all-done.1.s_ref = bf16[8,64,64,128]{3,2,1,0:T(8,128)(2,1)} async-done(((bf16[8,64,64,128]{3,2,1,0:T(8,128)(2,1)}), bf16[8,64,64,128]{3,2,1,0:T(8,128)(2,1)}, u32[]{:S(2)}, u32[]{:S(2)}) %all-to-all-start.1) | async-done | bytes 8388640 | tf_op jit(solution)/shard_map/all_to_all | solution.py:195
  200.3 5.2 all-to-all-start
  205.5 0.0 copy-done.4
  205.5 1.0 copy.19
  206.5 0.0 copy-done
  206.5 0.6 constant_dynamic-slice_fusion.gate_one_ref
  207.1 33.2 %middle.2 = (bf16[512,64,256]{2,1,0:T(8,128)(2,1)}, bf16[8,64,64,128]{3,2,1,0:T(8,128)(2,1)}, f32[512,512]{1,0:T(8,128)}, f32[64,128]{1,0:T(8,128)}, f32[512,128]{1,0:T(8,128)}) custom-call(bf16[512,512]{1,0:T(8,128)(2,1)} %left_ref.3, bf16[512,512]{1,0:T(8,128)(2,1)} %bitcast.36, bf16[8,64,64,128]{3,2,1,0:T(8,128)(2,1)} %all-to-all-done.1.s_ref, ...), custom_call_target="tpu_custom_call" | custom-call | flops 12884901888 | bytes 33554432 | tf_op jit(solution)/shard_map/middle/pallas_call | solution.py:270
  240.4 147.1 %all-to-all-done.s_ref = bf16[8,64,64,128]{3,2,1,0:T(8,128)(2,1)} async-done(((bf16[8,64,64,128]{3,2,1,0:T(8,128)(2,1)}), bf16[8,64,64,128]{3,2,1,0:T(8,128)(2,1)}, u32[]{:S(2)}, u32[]{:S(2)}) %all-to-all-start) | async-done | bytes 8388640 | tf_op jit(solution)/shard_map/all_to_all | solution.py:195
  387.5 5.2 all-to-all-start.3
  392.7 33.3 %middle.3 = (bf16[512,64,256]{2,1,0:T(8,128)(2,1)}, bf16[8,64,64,128]{3,2,1,0:T(8,128)(2,1)}, f32[512,512]{1,0:T(8,128)}, f32[64,128]{1,0:T(8,128)}, f32[512,128]{1,0:T(8,128)}) custom-call(bf16[512,512]{1,0:T(8,128)(2,1)} %left_ref.3, bf16[512,512]{1,0:T(8,128)(2,1)} %bitcast.37, ...), custom_call_target="tpu_custom_call", output_to_operand_aliasing={{0}: (6, {})} | custom-call | flops 12884901888 | bytes 33554432 | tf_op jit(solution)/shard_map/middle/pallas_call | solution.py:270
  426.0 148.7 %all-to-all-done.3.g_ref = bf16[8,64,64,128]{3,2,1,0:T(8,128)(2,1)} async-done(((bf16[8,64,64,128]{3,2,1,0:T(8,128)(2,1)}), bf16[8,64,64,128]{3,2,1,0:T(8,128)(2,1)}, u32[]{:S(2)}, u32[]{:S(2)}) %all-to-all-start.3) | async-done | bytes 8388640 | tf_op jit(solution)/shard_map/all_to_all | solution.py:195
  574.6 0.0 copy-start.3
  574.6 5.4 all-to-all-start.2
  580.1 0.0 copy-start.2
  580.1 0.0 copy-start.5
  580.1 0.0 copy-start.6
  580.2 0.0 copy-done.3
  580.2 1.5 add.48
  581.7 0.8 dynamic-slice_bitcast_fusion.2
  582.4 0.0 collective-permute-start.2
  582.4 1.5 collective-permute-start.1
  584.0 0.3 collective-permute-start
  584.3 1.1 pad_maximum_fusion
  585.4 0.3 concatenate.16
  585.7 5.5 collective-permute-done.2
  591.2 5.8 collective-permute-done.1
  597.0 0.0 collective-permute-done
  597.0 1.1 fusion.2
  598.1 0.2 concatenate.14
  598.3 0.2 copy_dynamic-update-slice_fusion.1
  598.5 0.4 copy_dynamic-update-slice_fusion
  598.9 0.1 fusion.3
  599.0 1.7 collective-permute-start.3
  600.6 0.0 copy-done.2
  600.6 1.0 copy.22
  601.6 0.0 copy-done.5
  601.6 0.0 copy-done.6
  601.7 0.6 pad_maximum_fusion.1
  602.3 50.7 %collective-permute-done.3 = bf16[4,24576]{1,0:T(4,128)(2,1)S(1)} collective-permute-done((bf16[4,24576]{1,0:T(4,128)(2,1)S(1)}, bf16[4,24576]{1,0:T(4,128)(2,1)S(1)}, u32[]{:S(2)}, u32[]{:S(2)}) %collective-permute-start.3) | collective-permute-done | bytes 196640 | tf_op jit(solution)/shard_map/ppermute | solution.py:330
  653.0 0.1 fusion.4
  653.1 0.7 copy.27
  653.8 1.1 broadcast_in_dim.3.start_ref
  654.9 9.1 %grad_right.2.start_ref = f32[512,512]{1,0:T(8,128)} custom-call(bf16[8,64,64,128]{3,2,1,0:T(8,128)(2,1)} %all-to-all-done.3.g_ref, bf16[64,512,256]{2,1,0:T(8,128)(2,1)} %x_ref.7, f32[512,512]{1,0:T(8,128)} %broadcast_in_dim.3.start_ref), custom_call_target="tpu_custom_call" | custom-call | flops 4294967296 | bytes 16777216 | tf_op jit(solution)/shard_map/grad_right/pallas_call | solution.py:107
  664.0 11.0 %grad_inputs.2.refs_0_ = bf16[64,512,256]{2,1,0:T(8,128)(2,1)} custom-call(bf16[512,512]{1,0:T(8,128)(2,1)} %bitcast.31, bf16[8,64,64,128]{3,2,1,0:T(8,128)(2,1)} %all-to-all-done.3.g_ref), custom_call_target="tpu_custom_call" | custom-call | flops 4294967296 | bytes 16777216 | tf_op jit(solution)/shard_map/grad_inputs/pallas_call | solution.py:158
  675.0 87.2 %all-to-all-done.2.g_ref = bf16[8,64,64,128]{3,2,1,0:T(8,128)(2,1)} async-done(((bf16[8,64,64,128]{3,2,1,0:T(8,128)(2,1)}), bf16[8,64,64,128]{3,2,1,0:T(8,128)(2,1)}, u32[]{:S(2)}, u32[]{:S(2)}) %all-to-all-start.2) | async-done | bytes 8388640 | tf_op jit(solution)/shard_map/all_to_all | solution.py:195
  762.2 4.0 all-to-all-start.5
  766.2 8.8 %grad_right.3 = bf16[512,512]{1,0:T(8,128)(2,1)} custom-call(bf16[8,64,64,128]{3,2,1,0:T(8,128)(2,1)} %all-to-all-done.2.g_ref, bf16[64,512,256]{2,1,0:T(8,128)(2,1)} %x_ref.7, f32[512,512]{1,0:T(8,128)} %grad_right.2.start_ref), custom_call_target="tpu_custom_call" | custom-call | flops 4294967296 | bytes 16777216 | tf_op jit(solution)/shard_map/grad_right/pallas_call | solution.py:107
  775.0 0.0 all-to-all-done.5
  775.0 5.2 all-to-all-start.4
  780.3 0.0 copy-start.1
  780.3 11.0 %grad_inputs.3 = bf16[64,512,256]{2,1,0:T(8,128)(2,1)} custom-call(bf16[512,512]{1,0:T(8,128)(2,1)} %bitcast.32, bf16[8,64,64,128]{3,2,1,0:T(8,128)(2,1)} %all-to-all-done.2.g_ref, bf16[64,512,256]{2,1,0:T(8,128)(2,1)} %grad_inputs.2.refs_0_), custom_call_target="tpu_custom_call", output_to_operand_aliasing={{}: (2, {})} | custom-call | flops 4294967296 | bytes 16777216 | tf_op jit(solution)/shard_map/grad_inputs/pallas_call | solution.py:158
  791.4 0.6 reshape.55
  792.0 0.6 reshape.56
  792.7 3.2 all-to-all-done.4
  795.8 0.7 convert_reduce_fusion
  796.5 0.0 copy-done.1
  (3 shorter events, 0.0 us)
Async XLA Ops:
  0.6 205.9 %copy-start = (bf16[512,256]{1,0:T(8,128)(2,1)S(1)}, bf16[512,256]{1,0:T(8,128)(2,1)}, u32[]{:S(2)}) copy-start(bf16[512,256]{1,0:T(8,128)(2,1)} %param.10) | copy-start | bytes 786436
  9.8 190.5 %all-to-all-start.1 = ((bf16[8,64,64,128]{3,2,1,0:T(8,128)(2,1)}), bf16[8,64,64,128]{3,2,1,0:T(8,128)(2,1)}, u32[]{:S(2)}, u32[]{:S(2)}) async-start(bf16[8,64,64,128]{3,2,1,0:T(8,128)(2,1)} %section_one.3), calls=%async_computation.1 | async-start | bytes 16777216 | tf_op jit(solution)/shard_map/all_to_all | solution.py:195
  26.2 179.3 %copy-start.4 = (bf16[512,512]{1,0:T(8,128)(2,1)S(1)}, bf16[512,512]{1,0:T(8,128)(2,1)}, u32[]{:S(2)}) copy-start(bf16[512,512]{1,0:T(8,128)(2,1)} %left_ref.3) | copy-start | bytes 1572868
  200.3 187.2 %all-to-all-start = ((bf16[8,64,64,128]{3,2,1,0:T(8,128)(2,1)}), bf16[8,64,64,128]{3,2,1,0:T(8,128)(2,1)}, u32[]{:S(2)}, u32[]{:S(2)}) async-start(bf16[8,64,64,128]{3,2,1,0:T(8,128)(2,1)} %section_one.2), calls=%async_computation | async-start | bytes 16777216 | tf_op jit(solution)/shard_map/all_to_all | solution.py:195
  387.5 187.1 %all-to-all-start.3 = ((bf16[8,64,64,128]{3,2,1,0:T(8,128)(2,1)}), bf16[8,64,64,128]{3,2,1,0:T(8,128)(2,1)}, u32[]{:S(2)}, u32[]{:S(2)}) async-start(bf16[8,64,64,128]{3,2,1,0:T(8,128)(2,1)} %get-tuple-element.31), calls=%async_computation.3 | async-start | bytes 16777216 | tf_op jit(solution)/shard_map/all_to_all | solution.py:195
  574.6 5.5 copy-start.3
  574.6 187.6 %all-to-all-start.2 = ((bf16[8,64,64,128]{3,2,1,0:T(8,128)(2,1)}), bf16[8,64,64,128]{3,2,1,0:T(8,128)(2,1)}, u32[]{:S(2)}, u32[]{:S(2)}) async-start(bf16[8,64,64,128]{3,2,1,0:T(8,128)(2,1)} %get-tuple-element.24), calls=%async_computation.2 | async-start | bytes 16777216 | tf_op jit(solution)/shard_map/all_to_all | solution.py:195
  580.1 20.5 %copy-start.2 = (bf16[512,512]{1,0:T(8,128)(2,1)S(1)}, bf16[512,512]{1,0:T(8,128)(2,1)}, u32[]{:S(2)}) copy-start(bf16[512,512]{1,0:T(8,128)(2,1)} %w_ref.3) | copy-start | bytes 1572868
  580.1 21.5 %copy-start.5 = (f32[64,128]{1,0:T(8,128)S(1)}, f32[64,128]{1,0:T(8,128)}, u32[]{:S(2)}) copy-start(f32[64,128]{1,0:T(8,128)} %get-tuple-element.29) | copy-start | bytes 98308
  580.1 21.5 %copy-start.6 = (f32[64,128]{1,0:T(8,128)S(1)}, f32[64,128]{1,0:T(8,128)}, u32[]{:S(2)}) copy-start(f32[64,128]{1,0:T(8,128)} %get-tuple-element.30) | copy-start | bytes 98308
  582.4 8.8 %collective-permute-start.2 = (f32[1,8,16,512]{3,2,1,0:T(8,128)}, f32[1,8,16,512]{3,2,1,0:T(8,128)S(1)}, u32[]{:S(2)}, u32[]{:S(2)}) collective-permute-start(f32[1,8,16,512]{3,2,1,0:T(8,128)} %get-tuple-element.39), channel_id=1, source_target_pairs={{0,3},{1,2},{2,1},{3,0},{4,7},{5,6},{6,5},{7,4},{8,11},{9,10},{10,... | collective-permute-start | bytes 786440 | tf_op jit(solution)/shard_map/ppermute | solution.py:189
  582.4 14.5 %collective-permute-start.1 = (f32[1,8,16,512]{3,2,1,0:T(8,128)S(1)}, f32[1,8,16,512]{3,2,1,0:T(8,128)}, u32[]{:S(2)}, u32[]{:S(2)}) collective-permute-start(f32[1,8,16,512]{3,2,1,0:T(8,128)S(1)} %get-tuple-element.40), channel_id=1, source_target_pairs={{0,2},{1,3},{2,0},{3,1},{4,6},{5,7},{6,4},{7,5},{8,10},{9,11},{10,... | collective-permute-start | bytes 786440 | tf_op jit(solution)/shard_map/ppermute | solution.py:189
  584.0 13.0 %collective-permute-start = (f32[1,8,16,512]{3,2,1,0:T(8,128)S(1)}, f32[1,8,16,512]{3,2,1,0:T(8,128)}, u32[]{:S(2)}, u32[]{:S(2)}) collective-permute-start(f32[1,8,16,512]{3,2,1,0:T(8,128)S(1)} %get-tuple-element.38), channel_id=1, source_target_pairs={{0,1},{1,0},{2,3},{3,2},{4,5},{5,4},{6,7},{7,6},{8,9},{9,8},{10,11... | collective-permute-start | bytes 786440 | tf_op jit(solution)/shard_map/ppermute | solution.py:189
  599.0 54.0 %collective-permute-start.3 = (bf16[4,24576]{1,0:T(4,128)(2,1)S(1)}, bf16[4,24576]{1,0:T(4,128)(2,1)S(1)}, u32[]{:S(2)}, u32[]{:S(2)}) collective-permute-start(bf16[4,24576]{1,0:T(4,128)(2,1)S(1)} %fusion.3), channel_id=1, source_target_pairs={{0,4},{4,0},{8,12},{12,8},{16,20},{20,16},{24,28},{28,24},{1,5},{5... | collective-permute-start | bytes 589832 | tf_op jit(solution)/shard_map/ppermute | solution.py:330
  762.2 12.8 %all-to-all-start.5 = ((bf16[4,192,128]{2,1,0:T(8,128)(2,1)}), bf16[4,192,128]{2,1,0:T(8,128)(2,1)S(1)}, u32[]{:S(2)}, u32[]{:S(2)}) async-start(bf16[4,192,128]{2,1,0:T(8,128)(2,1)} %bitcast.30), calls=%async_computation.5 | async-start | bytes 393216 | tf_op jit(solution)/shard_map/all_to_all | solution.py:195
  775.0 20.8 %all-to-all-start.4 = ((bf16[32,16,512]{2,1,0:T(8,128)(2,1)}), bf16[32,16,512]{2,1,0:T(8,128)(2,1)S(1)}, u32[]{:S(2)}, u32[]{:S(2)}) async-start(bf16[32,16,512]{2,1,0:T(8,128)(2,1)} %bitcast.35), calls=%async_computation.4 | async-start | bytes 1048576 | tf_op jit(solution)/shard_map/all_to_all | solution.py:352
  780.3 16.2 %copy-start.1 = (bf16[512,256]{1,0:T(8,128)(2,1)S(1)}, bf16[512,256]{1,0:T(8,128)(2,1)}, u32[]{:S(2)}) copy-start(bf16[512,256]{1,0:T(8,128)(2,1)} %param.10) | copy-start | bytes 786436

commit v4 on v3

--- a/solution.py
+++ b/solution.py
@@ -172,29 +172,30 @@
     )(*operands)
 
 
-def scatter_sum(blocks, axis, size, dtype):
+def scatter_step(blocks, axis, size, low, radix, dtype):
+    groups = blocks.reshape((blocks.shape[0] // radix, radix) + blocks.shape[1:])
+    mine = (lax.axis_index(axis) // low) % radix
+    blocks = lax.dynamic_index_in_dim(groups, mine, axis=1, keepdims=False)
+    groups = groups.astype(dtype)
+    for d in range(1, radix):
+        sent = lax.dynamic_index_in_dim(groups, mine ^ d, axis=1, keepdims=False)
+        pairs = [(s, s ^ (d * low)) for s in range(size)]
+        blocks = blocks + lax.ppermute(sent, axis, pairs).astype(F32)
+    return blocks
+
+
+def scatter_sum(blocks, axis, size, dtype, low=1):
     if size & (size - 1):
         return lax.psum_scatter(blocks, axis, scatter_dimension=0)
-    index = lax.axis_index(axis)
-    low = 1
     while low < size:
         radix = min(8, size // low)
-        groups = blocks.reshape((blocks.shape[0] // radix, radix) + blocks.shape[1:])
-        mine = (index // low) % radix
-        blocks = lax.dynamic_index_in_dim(groups, mine, axis=1, keepdims=False)
-        groups = groups.astype(dtype)
-        for d in range(1, radix):
-            sent = lax.dynamic_index_in_dim(groups, mine ^ d, axis=1, keepdims=False)
-            pairs = [(s, s ^ (d * low)) for s in range(size)]
-            blocks = blocks + lax.ppermute(sent, axis, pairs).astype(F32)
+        blocks = scatter_step(blocks, axis, size, low, radix, dtype)
         low *= radix
     return blocks[0]
 
 
-def exchange(blocks, groups=None):
-    return lax.all_to_all(
-        blocks, "seq", split_axis=0, concat_axis=0, tiled=True, axis_index_groups=groups
-    )
+def exchange(blocks):
+    return lax.all_to_all(blocks, "seq", split_axis=0, concat_axis=0, tiled=True)
 
 
 def middle_kernel(
@@ -322,16 +323,10 @@
     size = grad_left.size // n
     grad_second = jnp.concatenate(seconds, axis=1)
     both = jnp.concatenate([grad_left.reshape(n, -1), grad_second.reshape(n, -1)], axis=1)
-    if n % 2 == 0:
-        me = lax.axis_index("seq") % 2
-        pairs = both.reshape(n // 2, 2, -1)
-        sent = lax.dynamic_index_in_dim(pairs, 1 - me, axis=1, keepdims=False).astype(BF16)
-        both = lax.dynamic_index_in_dim(pairs, me, axis=1, keepdims=False)
-        both = both + lax.ppermute(sent, "seq", [(s, s ^ 1) for s in range(n)]).astype(F32)
-        groups = [list(range(b, n, 2)) for b in range(2)]
-    else:
-        groups = None
-    both = both.astype(BF16).reshape(both.shape[0], -1, LANES)
+    low = 1
+    if n > 2 and n & (n - 1) == 0:
+        both = scatter_step(both, "seq", n, 1, 2, BF16)
+        low = 2
 
     right_t = right_weight.T
     grad_first = jnp.concatenate(firsts, axis=1)
@@ -341,18 +336,18 @@
         terms = grad_right_terms(returned[h], inputs, h, terms, F32)
         grad_inputs = grad_inputs_half(right_t, returned[h], h, channels, grad_inputs)
     h = halves - 1
-    returned[h], both, grad_first, terms, grad_inputs, right_t = lax.optimization_barrier(
-        (returned[h], both, grad_first, terms, grad_inputs, right_t)
+    returned[h], grad_first, terms, grad_inputs, right_t = lax.optimization_barrier(
+        (returned[h], grad_first, terms, grad_inputs, right_t)
     )
-    both = exchange(both, groups)
-    both = jnp.sum(both.astype(F32), axis=0).reshape(-1)
-    grad_left = both[:size].reshape(-1, left_weight.shape[1])
-    grad_second = both[size:].reshape(-1, channels)
     terms = grad_right_terms(returned[h], inputs, h, terms, BF16)
+    terms, both = lax.optimization_barrier((terms, both))
     terms = lax.all_to_all(
         terms.reshape(n * m, -1, cols), ("seq", "ch"), split_axis=0, concat_axis=0, tiled=True
     )
     grad_right = jnp.sum(terms.astype(F32), axis=0)
+    both = scatter_sum(both, "seq", n, BF16, low)
+    grad_left = both[:size].reshape(-1, left_weight.shape[1])
+    grad_second = both[size:].reshape(-1, channels)
     grad_inputs = grad_inputs_half(right_t, returned[h], h, channels, grad_inputs)
     return output, grad_inputs, grad_right, grad_left, grad_first, grad_second
 

time: 798 us -> 797 us (level)
    ppermute x4 -> x7, waiting for transfers between devices: 61.9 us -> 67.6 us  [scatter_step(): blocks = blocks + lax.ppermute(sent, axis, pairs).astype(F32)]
    all_to_all x5 -> x4, waiting for transfers between devices: 557 us -> 553 us  [exchange(): lax.all_to_all(blocks, 'seq', split_axis=0, concat_axis=0, tiled=True)]
    all_to_all x5 -> x4, starting transfers between devices: 27.1 us -> 23.1 us  [exchange(): lax.all_to_all(blocks, 'seq', split_axis=0, concat_axis=0, tiled=True)]
  transfers between devices with their start and end apart: 10 -> 12, of which waited for: 8 -> 6; matrix products, arithmetic and copies ran while one was open for 2% -> 1% of each run, Pallas kernels for 15% -> 13%
where the time goes in v4:
time: 797 us; the launch traced here: 796 us
  waiting for transfers between devices  623 us (78%)
  Pallas kernels  125 us (16%)
  starting transfers between devices  35.1 us (4%)
    all_to_all x4, waiting for transfers between devices, exchange(): lax.all_to_all(blocks, 'seq', split_axis=0, concat_axis=0, tiled=True)  553 us
    ppermute x7, waiting for transfers between devices, scatter_step(): blocks = blocks + lax.ppermute(sent, axis, pairs).astype(F32)  67.6 us
    pallas_call x2, Pallas kernels, middle(): pl.pallas_call(middle_kernel, grid=(share // step,), in_specs=in_specs, o...  66.6 us
    all_to_all x4, starting transfers between devices, exchange(): lax.all_to_all(blocks, 'seq', split_axis=0, concat_axis=0, tiled=True)  23.1 us
    pallas_call x2, Pallas kernels, grad_inputs_half(): pl.pallas_call(inputs_kernel, grid=(rows // step,), in_specs=in_specs, ou...  22 us
    pallas_call x2, Pallas kernels, section_one(): pl.pallas_call(functools.partial(section_kernel, half, step), in_specs=[p...  18.2 us
    pallas_call x2, Pallas kernels, grad_right_terms(): pl.pallas_call(functools.partial(right_kernel, half, step), in_specs=[pl....  17.9 us
  transfers between devices with their start and end apart: 12, of which 6 were waited for; matrix products, arithmetic and copies ran while one was open for 1% of the time, Pallas kernels for 13%

profile of v4, /device:TPU:0, one launch (start us, length us, event | category | flops | bytes accessed | tf_op | source)
XLA Modules:
  0.0 796.1 jit_solution(13694376799928454935)
XLA Ops:
  0.6 0.0 copy-start
  0.6 9.1 %section_one.3 = bf16[8,64,64,128]{3,2,1,0:T(8,128)(2,1)} custom-call(bf16[512,512]{1,0:T(8,128)(2,1)} %w_ref.3, bf16[64,512,256]{2,1,0:T(8,128)(2,1)} %x_ref.7), custom_call_target="tpu_custom_call" | custom-call | flops 4294967296 | bytes 16777216 | tf_op jit(solution)/shard_map/section_one/pallas_call | solution.py:46
  9.8 7.3 all-to-all-start.1
  17.1 9.1 %section_one.2 = bf16[8,64,64,128]{3,2,1,0:T(8,128)(2,1)} custom-call(bf16[512,512]{1,0:T(8,128)(2,1)} %w_ref.3, bf16[64,512,256]{2,1,0:T(8,128)(2,1)} %x_ref.7), custom_call_target="tpu_custom_call" | custom-call | flops 4294967296 | bytes 16777216 | tf_op jit(solution)/shard_map/section_one/pallas_call | solution.py:46
  26.2 0.0 copy-start.4
  26.2 174.0 %all-to-all-done.1.s_ref = bf16[8,64,64,128]{3,2,1,0:T(8,128)(2,1)} async-done(((bf16[8,64,64,128]{3,2,1,0:T(8,128)(2,1)}), bf16[8,64,64,128]{3,2,1,0:T(8,128)(2,1)}, u32[]{:S(2)}, u32[]{:S(2)}) %all-to-all-start.1) | async-done | bytes 8388640 | tf_op jit(solution)/shard_map/all_to_all | solution.py:198
  200.3 5.2 all-to-all-start
  205.5 0.0 copy-done.4
  205.5 1.0 copy.19
  206.5 0.0 copy-done
  206.5 0.6 constant_dynamic-slice_fusion.3.gate_one_ref
  207.1 33.2 %middle.2 = (bf16[512,64,256]{2,1,0:T(8,128)(2,1)}, bf16[8,64,64,128]{3,2,1,0:T(8,128)(2,1)}, f32[512,512]{1,0:T(8,128)}, f32[64,128]{1,0:T(8,128)}, f32[512,128]{1,0:T(8,128)}) custom-call(bf16[512,512]{1,0:T(8,128)(2,1)} %left_ref.3, bf16[512,512]{1,0:T(8,128)(2,1)} %bitcast.27, bf16[8,64,64,128]{3,2,1,0:T(8,128)(2,1)} %all-to-all-done.1.s_ref, ...), custom_call_target="tpu_custom_call" | custom-call | flops 12884901888 | bytes 33554432 | tf_op jit(solution)/shard_map/middle/pallas_call | solution.py:271
  240.4 147.1 %all-to-all-done.s_ref = bf16[8,64,64,128]{3,2,1,0:T(8,128)(2,1)} async-done(((bf16[8,64,64,128]{3,2,1,0:T(8,128)(2,1)}), bf16[8,64,64,128]{3,2,1,0:T(8,128)(2,1)}, u32[]{:S(2)}, u32[]{:S(2)}) %all-to-all-start) | async-done | bytes 8388640 | tf_op jit(solution)/shard_map/all_to_all | solution.py:198
  387.5 5.2 all-to-all-start.3
  392.7 0.0 copy-start.3
  392.7 0.0 copy-start.5
  392.7 33.4 %middle.3 = (bf16[512,64,256]{2,1,0:T(8,128)(2,1)}, bf16[8,64,64,128]{3,2,1,0:T(8,128)(2,1)}, f32[512,512]{1,0:T(8,128)}, f32[64,128]{1,0:T(8,128)}, f32[512,128]{1,0:T(8,128)}) custom-call(bf16[512,512]{1,0:T(8,128)(2,1)} %left_ref.3, bf16[512,512]{1,0:T(8,128)(2,1)} %bitcast.28, ...), custom_call_target="tpu_custom_call", output_to_operand_aliasing={{0}: (6, {})} | custom-call | flops 12884901888 | bytes 33554432 | tf_op jit(solution)/shard_map/middle/pallas_call | solution.py:271
  426.1 1.4 add.76
  427.6 0.1 dynamic-slice_bitcast_fusion.2
  427.7 0.1 collective-permute-start
  427.7 1.6 collective-permute-start.1
  429.3 0.3 collective-permute-start.2
  429.6 1.0 pad_maximum_fusion
  430.6 0.3 concatenate.17
  431.0 143.7 %all-to-all-done.3.g_ref = bf16[8,64,64,128]{3,2,1,0:T(8,128)(2,1)} async-done(((bf16[8,64,64,128]{3,2,1,0:T(8,128)(2,1)}), bf16[8,64,64,128]{3,2,1,0:T(8,128)(2,1)}, u32[]{:S(2)}, u32[]{:S(2)}) %all-to-all-start.3) | async-done | bytes 8388640 | tf_op jit(solution)/shard_map/all_to_all | solution.py:198
  574.6 5.4 all-to-all-start.2
  580.0 0.0 collective-permute-done
  580.0 0.0 collective-permute-done.1
  580.0 0.0 collective-permute-done.2
  580.0 1.0 fusion.1
  581.1 0.2 concatenate.15
  581.3 0.2 copy_dynamic-update-slice_fusion.1
  581.5 0.4 copy_dynamic-update-slice_fusion
  581.9 0.1 fusion.2
  581.9 1.7 collective-permute-start.3
  583.6 1.0 copy.20
  584.6 0.0 copy-done.7
  584.6 0.6 pad_maximum_fusion.1
  585.3 67.6 %collective-permute-done.3 = bf16[4,24576]{1,0:T(4,128)(2,1)S(1)} collective-permute-done((bf16[4,24576]{1,0:T(4,128)(2,1)S(1)}, bf16[4,24576]{1,0:T(4,128)(2,1)S(1)}, u32[]{:S(2)}, u32[]{:S(2)}) %collective-permute-start.3) | collective-permute-done | bytes 196640 | tf_op jit(solution)/shard_map/ppermute | solution.py:183
  652.9 0.1 bitcast_add_fusion
  653.0 11.0 %grad_inputs.2.refs_0_ = bf16[64,512,256]{2,1,0:T(8,128)(2,1)} custom-call(bf16[512,512]{1,0:T(8,128)(2,1)} %bitcast.22, bf16[8,64,64,128]{3,2,1,0:T(8,128)(2,1)} %all-to-all-done.3.g_ref), custom_call_target="tpu_custom_call" | custom-call | flops 4294967296 | bytes 16777216 | tf_op jit(solution)/shard_map/grad_inputs/pallas_call | solution.py:158
  664.0 1.1 broadcast_in_dim.3.start_ref
  665.1 9.1 %grad_right.2.start_ref = f32[512,512]{1,0:T(8,128)} custom-call(bf16[8,64,64,128]{3,2,1,0:T(8,128)(2,1)} %all-to-all-done.3.g_ref, bf16[64,512,256]{2,1,0:T(8,128)(2,1)} %x_ref.7, f32[512,512]{1,0:T(8,128)} %broadcast_in_dim.3.start_ref), custom_call_target="tpu_custom_call" | custom-call | flops 4294967296 | bytes 16777216 | tf_op jit(solution)/shard_map/grad_right/pallas_call | solution.py:107
  674.2 88.0 %all-to-all-done.2.g_ref = bf16[8,64,64,128]{3,2,1,0:T(8,128)(2,1)} async-done(((bf16[8,64,64,128]{3,2,1,0:T(8,128)(2,1)}), bf16[8,64,64,128]{3,2,1,0:T(8,128)(2,1)}, u32[]{:S(2)}, u32[]{:S(2)}) %all-to-all-start.2) | async-done | bytes 8388640 | tf_op jit(solution)/shard_map/all_to_all | solution.py:198
  762.2 8.8 %grad_right.3 = bf16[512,512]{1,0:T(8,128)(2,1)} custom-call(bf16[8,64,64,128]{3,2,1,0:T(8,128)(2,1)} %all-to-all-done.2.g_ref, bf16[64,512,256]{2,1,0:T(8,128)(2,1)} %x_ref.7, f32[512,512]{1,0:T(8,128)} %grad_right.2.start_ref), custom_call_target="tpu_custom_call" | custom-call | flops 4294967296 | bytes 16777216 | tf_op jit(solution)/shard_map/grad_right/pallas_call | solution.py:107
  771.0 0.1 convert_element_type.25
  771.1 0.3 constant_dynamic-slice_fusion.2
  771.4 0.1 collective-permute-start.4
  771.5 3.2 collective-permute-start.5
  774.8 1.1 collective-permute-start.6
  775.9 4.0 all-to-all-start.4
  779.9 0.0 copy-start.1
  779.9 11.0 %grad_inputs.3 = bf16[64,512,256]{2,1,0:T(8,128)(2,1)} custom-call(bf16[512,512]{1,0:T(8,128)(2,1)} %bitcast.23, bf16[8,64,64,128]{3,2,1,0:T(8,128)(2,1)} %all-to-all-done.2.g_ref, bf16[64,512,256]{2,1,0:T(8,128)(2,1)} %grad_inputs.2.refs_0_), custom_call_target="tpu_custom_call", output_to_operand_aliasing={{}: (2, {})} | custom-call | flops 4294967296 | bytes 16777216 | tf_op jit(solution)/shard_map/grad_inputs/pallas_call | solution.py:158
  790.9 0.0 collective-permute-done.4
  790.9 0.0 collective-permute-done.5
  790.9 0.0 collective-permute-done.6
  791.0 0.2 convert_add_fusion
  791.2 0.2 slice_reduce_fusion
  791.4 0.6 reshape.60
  792.0 0.1 slice_reduce_fusion.1
  792.1 0.6 reshape.59
  792.7 2.7 all-to-all-done.4
  795.4 0.7 convert_reduce_fusion
  796.1 0.0 copy-done.1
  (7 shorter events, 0.0 us)
Async XLA Ops:
  0.6 205.9 %copy-start = (bf16[512,256]{1,0:T(8,128)(2,1)S(1)}, bf16[512,256]{1,0:T(8,128)(2,1)}, u32[]{:S(2)}) copy-start(bf16[512,256]{1,0:T(8,128)(2,1)} %param.10) | copy-start | bytes 786436
  9.8 190.5 %all-to-all-start.1 = ((bf16[8,64,64,128]{3,2,1,0:T(8,128)(2,1)}), bf16[8,64,64,128]{3,2,1,0:T(8,128)(2,1)}, u32[]{:S(2)}, u32[]{:S(2)}) async-start(bf16[8,64,64,128]{3,2,1,0:T(8,128)(2,1)} %section_one.3), calls=%async_computation.1 | async-start | bytes 16777216 | tf_op jit(solution)/shard_map/all_to_all | solution.py:198
  26.2 179.3 %copy-start.4 = (bf16[512,512]{1,0:T(8,128)(2,1)S(1)}, bf16[512,512]{1,0:T(8,128)(2,1)}, u32[]{:S(2)}) copy-start(bf16[512,512]{1,0:T(8,128)(2,1)} %left_ref.3) | copy-start | bytes 1572868
  200.3 187.2 %all-to-all-start = ((bf16[8,64,64,128]{3,2,1,0:T(8,128)(2,1)}), bf16[8,64,64,128]{3,2,1,0:T(8,128)(2,1)}, u32[]{:S(2)}, u32[]{:S(2)}) async-start(bf16[8,64,64,128]{3,2,1,0:T(8,128)(2,1)} %section_one.2), calls=%async_computation | async-start | bytes 16777216 | tf_op jit(solution)/shard_map/all_to_all | solution.py:198
  387.5 187.1 %all-to-all-start.3 = ((bf16[8,64,64,128]{3,2,1,0:T(8,128)(2,1)}), bf16[8,64,64,128]{3,2,1,0:T(8,128)(2,1)}, u32[]{:S(2)}, u32[]{:S(2)}) async-start(bf16[8,64,64,128]{3,2,1,0:T(8,128)(2,1)} %get-tuple-element.28), calls=%async_computation.3 | async-start | bytes 16777216 | tf_op jit(solution)/shard_map/all_to_all | solution.py:198
  392.7 33.4 %copy-start.3 = (f32[512,512]{1,0:T(8,128)S(1)}, f32[512,512]{1,0:T(8,128)}, u32[]{:S(2)}) copy-start(f32[512,512]{1,0:T(8,128)} %get-tuple-element.33) | copy-start | bytes 3145732
  392.7 36.9 %copy-start.5 = (f32[512,128]{1,0:T(8,128)S(1)}, f32[512,128]{1,0:T(8,128)}, u32[]{:S(2)}) copy-start(f32[512,128]{1,0:T(8,128)} %get-tuple-element.35) | copy-start | bytes 786436
  427.7 152.3 %collective-permute-start = (f32[1,8,16,512]{3,2,1,0:T(8,128)S(1)}, f32[1,8,16,512]{3,2,1,0:T(8,128)S(1)}, u32[]{:S(2)}, u32[]{:S(2)}) collective-permute-start(f32[1,8,16,512]{3,2,1,0:T(8,128)S(1)} %get-tuple-element.40), channel_id=1, source_target_pairs={{0,1},{1,0},{2,3},{3,2},{4,5},{5,4},{6,7},{7,6},{8,9},{9,8},{10,11... | collective-permute-start | bytes 786440 | tf_op jit(solution)/shard_map/ppermute | solution.py:183
  427.7 152.3 %collective-permute-start.1 = (f32[1,8,16,512]{3,2,1,0:T(8,128)S(1)}, f32[1,8,16,512]{3,2,1,0:T(8,128)S(1)}, u32[]{:S(2)}, u32[]{:S(2)}) collective-permute-start(f32[1,8,16,512]{3,2,1,0:T(8,128)S(1)} %get-tuple-element.42), channel_id=1, source_target_pairs={{0,2},{1,3},{2,0},{3,1},{4,6},{5,7},{6,4},{7,5},{8,10},{9,11},{10,... | collective-permute-start | bytes 786440 | tf_op jit(solution)/shard_map/ppermute | solution.py:183
  429.3 150.7 %collective-permute-start.2 = (f32[1,8,16,512]{3,2,1,0:T(8,128)S(1)}, f32[1,8,16,512]{3,2,1,0:T(8,128)}, u32[]{:S(2)}, u32[]{:S(2)}) collective-permute-start(f32[1,8,16,512]{3,2,1,0:T(8,128)S(1)} %get-tuple-element.41), channel_id=1, source_target_pairs={{0,3},{1,2},{2,1},{3,0},{4,7},{5,6},{6,5},{7,4},{8,11},{9,10},{10,... | collective-permute-start | bytes 786440 | tf_op jit(solution)/shard_map/ppermute | solution.py:183
  574.6 9.0 %copy-start.2 = (bf16[512,512]{1,0:T(8,128)(2,1)S(1)}, bf16[512,512]{1,0:T(8,128)(2,1)}, u32[]{:S(2)}) copy-start(bf16[512,512]{1,0:T(8,128)(2,1)} %w_ref.3) | copy-start | bytes 1572868
  574.6 10.0 %copy-start.6 = (f32[64,128]{1,0:T(8,128)S(1)}, f32[64,128]{1,0:T(8,128)}, u32[]{:S(2)}) copy-start(f32[64,128]{1,0:T(8,128)} %get-tuple-element.26) | copy-start | bytes 98308
  574.6 10.0 %copy-start.7 = (f32[64,128]{1,0:T(8,128)S(1)}, f32[64,128]{1,0:T(8,128)}, u32[]{:S(2)}) copy-start(f32[64,128]{1,0:T(8,128)} %get-tuple-element.27) | copy-start | bytes 98308
  574.6 187.6 %all-to-all-start.2 = ((bf16[8,64,64,128]{3,2,1,0:T(8,128)(2,1)}), bf16[8,64,64,128]{3,2,1,0:T(8,128)(2,1)}, u32[]{:S(2)}, u32[]{:S(2)}) async-start(bf16[8,64,64,128]{3,2,1,0:T(8,128)(2,1)} %get-tuple-element.25), calls=%async_computation.2 | async-start | bytes 16777216 | tf_op jit(solution)/shard_map/all_to_all | solution.py:198
  581.9 70.9 %collective-permute-start.3 = (bf16[4,24576]{1,0:T(4,128)(2,1)S(1)}, bf16[4,24576]{1,0:T(4,128)(2,1)S(1)}, u32[]{:S(2)}, u32[]{:S(2)}) collective-permute-start(bf16[4,24576]{1,0:T(4,128)(2,1)S(1)} %fusion.2), channel_id=1, source_target_pairs={{0,4},{4,0},{8,12},{12,8},{16,20},{20,16},{24,28},{28,24},{1,5},{5... | collective-permute-start | bytes 589832 | tf_op jit(solution)/shard_map/ppermute | solution.py:183
  771.4 19.5 %collective-permute-start.4 = (bf16[1,24576]{1,0:T(2,128)(2,1)S(1)}, bf16[1,24576]{1,0:T(2,128)(2,1)S(1)}, u32[]{:S(2)}, u32[]{:S(2)}) collective-permute-start(bf16[1,24576]{1,0:T(2,128)(2,1)S(1)} %get-tuple-element.43), channel_id=1, source_target_pairs={{0,8},{4,12},{8,0},{12,4},{16,24},{20,28},{24,16},{28,20},{1,9},{5... | collective-permute-start | bytes 147464 | tf_op jit(solution)/shard_map/ppermute | solution.py:183
  771.5 19.4 %collective-permute-start.5 = (bf16[1,24576]{1,0:T(2,128)(2,1)S(1)}, bf16[1,24576]{1,0:T(2,128)(2,1)S(1)}, u32[]{:S(2)}, u32[]{:S(2)}) collective-permute-start(bf16[1,24576]{1,0:T(2,128)(2,1)S(1)} %get-tuple-element.45), channel_id=1, source_target_pairs={{0,16},{4,20},{8,24},{12,28},{16,0},{20,4},{24,8},{28,12},{1,17},{... | collective-permute-start | bytes 147464 | tf_op jit(solution)/shard_map/ppermute | solution.py:183
  774.8 16.2 %collective-permute-start.6 = (bf16[1,24576]{1,0:T(2,128)(2,1)S(1)}, bf16[1,24576]{1,0:T(2,128)(2,1)S(1)}, u32[]{:S(2)}, u32[]{:S(2)}) collective-permute-start(bf16[1,24576]{1,0:T(2,128)(2,1)S(1)} %get-tuple-element.44), channel_id=1, source_target_pairs={{0,24},{4,28},{8,16},{12,20},{16,8},{20,12},{24,0},{28,4},{1,25},{... | collective-permute-start | bytes 147464 | tf_op jit(solution)/shard_map/ppermute | solution.py:183
  775.9 19.5 %all-to-all-start.4 = ((bf16[32,16,512]{2,1,0:T(8,128)(2,1)}), bf16[32,16,512]{2,1,0:T(8,128)(2,1)S(1)}, u32[]{:S(2)}, u32[]{:S(2)}) async-start(bf16[32,16,512]{2,1,0:T(8,128)(2,1)} %bitcast.26), calls=%async_computation.4 | async-start | bytes 1048576 | tf_op jit(solution)/shard_map/all_to_all | solution.py:344
  779.9 16.2 %copy-start.1 = (bf16[512,256]{1,0:T(8,128)(2,1)S(1)}, bf16[512,256]{1,0:T(8,128)(2,1)}, u32[]{:S(2)}) copy-start(bf16[512,256]{1,0:T(8,128)(2,1)} %param.10) | copy-start | bytes 786436

commit v5 on v4

--- a/solution.py
+++ b/solution.py
@@ -141,13 +141,15 @@
             out_ref[first + p] = y[:, p * LANES : (p + 1) * LANES]
 
 
-def grad_inputs_half(right_t, g, half, channels, before):
+def grad_inputs_half(right_t, g, half, channels, before, piece=0, pieces=1):
     n, rows, share, _ = g.shape
     cols = n * share
     step = min(8, rows)
+    count = rows // step // pieces
+    skip = piece * count
     in_specs = [
         pl.BlockSpec((cols, cols), lambda i: (0, 0)),
-        pl.BlockSpec((n, step, share, LANES), lambda i: (0, i, 0, 0)),
+        pl.BlockSpec((n, step, share, LANES), lambda i: (0, i + skip, 0, 0)),
     ]
     operands = [right_t, g]
     aliases = {}
@@ -157,15 +159,15 @@
         aliases = {2: 0}
     return pl.pallas_call(
         inputs_kernel,
-        grid=(rows // step,),
+        grid=(count,),
         in_specs=in_specs,
-        out_specs=pl.BlockSpec((step, cols, LANES), lambda i: (i, 0, half)),
+        out_specs=pl.BlockSpec((step, cols, LANES), lambda i: (i + skip, 0, half)),
         out_shape=jax.ShapeDtypeStruct((rows, cols, channels), BF16),
         input_output_aliases=aliases,
         compiler_params=pltpu.CompilerParams(vmem_limit_bytes=VMEM_LIMIT),
         cost_estimate=pl.CostEstimate(
-            flops=2 * rows * cols * cols * LANES,
-            bytes_accessed=4 * rows * cols * LANES,
+            flops=2 * count * step * cols * cols * LANES,
+            bytes_accessed=4 * count * step * cols * LANES,
             transcendentals=0,
         ),
         name="grad_inputs",
@@ -340,15 +342,21 @@
         (returned[h], grad_first, terms, grad_inputs, right_t)
     )
     terms = grad_right_terms(returned[h], inputs, h, terms, BF16)
-    terms, both = lax.optimization_barrier((terms, both))
+    terms, returned[h] = lax.optimization_barrier((terms, returned[h]))
     terms = lax.all_to_all(
         terms.reshape(n * m, -1, cols), ("seq", "ch"), split_axis=0, concat_axis=0, tiled=True
     )
     grad_right = jnp.sum(terms.astype(F32), axis=0)
-    both = scatter_sum(both, "seq", n, BF16, low)
+    pieces = 2 if rows % 16 == 0 else 1
+    for piece in range(pieces):
+        grad_inputs = grad_inputs_half(
+            right_t, returned[h], h, channels, grad_inputs, piece, pieces
+        )
+        if piece == 0:
+            grad_inputs, both = lax.optimization_barrier((grad_inputs, both))
+            both = scatter_sum(both, "seq", n, BF16, low)
     grad_left = both[:size].reshape(-1, left_weight.shape[1])
     grad_second = both[size:].reshape(-1, channels)
-    grad_inputs = grad_inputs_half(right_t, returned[h], h, channels, grad_inputs)
     return output, grad_inputs, grad_right, grad_left, grad_first, grad_second
 
 

time: 797 us -> 810 us (1.016)
  waiting for transfers between devices: 623 us -> 634 us
    all_to_all x1, waiting for transfers between devices: 2.68 us -> 13.7 us  [per_device(): lax.all_to_all(terms.reshape(n * m, -1, cols), ('seq', 'ch'), split_axis=...]
    pallas_call x2 -> x3, Pallas kernels: 22 us -> 23.4 us  [grad_inputs_half(): pl.pallas_call(inputs_kernel, grid=(count,), in_specs=in_specs, out_specs...]
where the time goes in v5:
time: 810 us; the launch traced here: 809 us
  waiting for transfers between devices  634 us (78%)
  Pallas kernels  126 us (16%)
  starting transfers between devices  35.1 us (4%)
    all_to_all x4, waiting for transfers between devices, exchange(): lax.all_to_all(blocks, 'seq', split_axis=0, concat_axis=0, tiled=True)  553 us
    ppermute x7, waiting for transfers between devices, scatter_step(): blocks = blocks + lax.ppermute(sent, axis, pairs).astype(F32)  67.6 us
    pallas_call x2, Pallas kernels, middle(): pl.pallas_call(middle_kernel, grid=(share // step,), in_specs=in_specs, o...  66.6 us
    pallas_call x3, Pallas kernels, grad_inputs_half(): pl.pallas_call(inputs_kernel, grid=(count,), in_specs=in_specs, out_specs...  23.4 us
    all_to_all x4, starting transfers between devices, exchange(): lax.all_to_all(blocks, 'seq', split_axis=0, concat_axis=0, tiled=True)  23.1 us
    pallas_call x2, Pallas kernels, section_one(): pl.pallas_call(functools.partial(section_kernel, half, step), in_specs=[p...  18.2 us
    pallas_call x2, Pallas kernels, grad_right_terms(): pl.pallas_call(functools.partial(right_kernel, half, step), in_specs=[pl....  17.9 us
  transfers between devices with their start and end apart: 12, of which 6 were waited for; matrix products, arithmetic and copies ran while one was open for 1% of the time, Pallas kernels for 13%

profile of v5, /device:TPU:0, one launch (start us, length us, event | category | flops | bytes accessed | tf_op | source)
XLA Modules:
  0.0 808.5 jit_solution(4762408269031078717)
XLA Ops:
  0.6 0.0 copy-start
  0.6 9.1 %section_one.3 = bf16[8,64,64,128]{3,2,1,0:T(8,128)(2,1)} custom-call(bf16[512,512]{1,0:T(8,128)(2,1)} %w_ref.3, bf16[64,512,256]{2,1,0:T(8,128)(2,1)} %x_ref.7), custom_call_target="tpu_custom_call" | custom-call | flops 4294967296 | bytes 16777216 | tf_op jit(solution)/shard_map/section_one/pallas_call | solution.py:46
  9.8 7.3 all-to-all-start.1
  17.1 9.1 %section_one.2 = bf16[8,64,64,128]{3,2,1,0:T(8,128)(2,1)} custom-call(bf16[512,512]{1,0:T(8,128)(2,1)} %w_ref.3, bf16[64,512,256]{2,1,0:T(8,128)(2,1)} %x_ref.7), custom_call_target="tpu_custom_call" | custom-call | flops 4294967296 | bytes 16777216 | tf_op jit(solution)/shard_map/section_one/pallas_call | solution.py:46
  26.2 0.0 copy-start.4
  26.2 174.0 %all-to-all-done.1.s_ref = bf16[8,64,64,128]{3,2,1,0:T(8,128)(2,1)} async-done(((bf16[8,64,64,128]{3,2,1,0:T(8,128)(2,1)}), bf16[8,64,64,128]{3,2,1,0:T(8,128)(2,1)}, u32[]{:S(2)}, u32[]{:S(2)}) %all-to-all-start.1) | async-done | bytes 8388640 | tf_op jit(solution)/shard_map/all_to_all | solution.py:200
  200.3 5.2 all-to-all-start
  205.5 0.0 copy-done.4
  205.5 1.0 copy.20
  206.5 0.0 copy-done
  206.5 0.6 constant_dynamic-slice_fusion.3.gate_one_ref
  207.1 33.2 %middle.2 = (bf16[512,64,256]{2,1,0:T(8,128)(2,1)}, bf16[8,64,64,128]{3,2,1,0:T(8,128)(2,1)}, f32[512,512]{1,0:T(8,128)}, f32[64,128]{1,0:T(8,128)}, f32[512,128]{1,0:T(8,128)}) custom-call(bf16[512,512]{1,0:T(8,128)(2,1)} %left_ref.3, bf16[512,512]{1,0:T(8,128)(2,1)} %bitcast.27, bf16[8,64,64,128]{3,2,1,0:T(8,128)(2,1)} %all-to-all-done.1.s_ref, ...), custom_call_target="tpu_custom_call" | custom-call | flops 12884901888 | bytes 33554432 | tf_op jit(solution)/shard_map/middle/pallas_call | solution.py:273
  240.4 147.1 %all-to-all-done.s_ref = bf16[8,64,64,128]{3,2,1,0:T(8,128)(2,1)} async-done(((bf16[8,64,64,128]{3,2,1,0:T(8,128)(2,1)}), bf16[8,64,64,128]{3,2,1,0:T(8,128)(2,1)}, u32[]{:S(2)}, u32[]{:S(2)}) %all-to-all-start) | async-done | bytes 8388640 | tf_op jit(solution)/shard_map/all_to_all | solution.py:200
  387.5 5.2 all-to-all-start.3
  392.7 0.0 copy-start.3
  392.7 0.0 copy-start.5
  392.7 33.4 %middle.3 = (bf16[512,64,256]{2,1,0:T(8,128)(2,1)}, bf16[8,64,64,128]{3,2,1,0:T(8,128)(2,1)}, f32[512,512]{1,0:T(8,128)}, f32[64,128]{1,0:T(8,128)}, f32[512,128]{1,0:T(8,128)}) custom-call(bf16[512,512]{1,0:T(8,128)(2,1)} %left_ref.3, bf16[512,512]{1,0:T(8,128)(2,1)} %bitcast.28, ...), custom_call_target="tpu_custom_call", output_to_operand_aliasing={{0}: (6, {})} | custom-call | flops 12884901888 | bytes 33554432 | tf_op jit(solution)/shard_map/middle/pallas_call | solution.py:273
  426.1 0.0 copy-done.3
  426.1 1.4 add.76
  427.6 0.1 dynamic-slice_bitcast_fusion.2
  427.7 0.1 collective-permute-start
  427.7 1.6 collective-permute-start.1
  429.3 0.3 collective-permute-start.2
  429.6 1.0 pad_maximum_fusion
  430.6 0.3 concatenate.17
  431.0 143.7 %all-to-all-done.3.g_ref = bf16[8,64,64,128]{3,2,1,0:T(8,128)(2,1)} async-done(((bf16[8,64,64,128]{3,2,1,0:T(8,128)(2,1)}), bf16[8,64,64,128]{3,2,1,0:T(8,128)(2,1)}, u32[]{:S(2)}, u32[]{:S(2)}) %all-to-all-start.3) | async-done | bytes 8388640 | tf_op jit(solution)/shard_map/all_to_all | solution.py:200
  574.6 5.4 all-to-all-start.2
  580.0 0.0 collective-permute-done
  580.0 0.0 collective-permute-done.1
  580.0 0.0 collective-permute-done.2
  580.0 1.0 fusion.1
  581.1 0.2 concatenate.15
  581.3 0.2 copy_dynamic-update-slice_fusion.1
  581.5 0.4 copy_dynamic-update-slice_fusion
  581.9 0.1 fusion.2
  581.9 1.7 collective-permute-start.3
  583.6 0.0 copy-done.2
  583.6 1.0 copy.21
  584.6 0.6 pad_maximum_fusion.1
  585.3 67.6 %collective-permute-done.3 = bf16[4,24576]{1,0:T(4,128)(2,1)S(1)} collective-permute-done((bf16[4,24576]{1,0:T(4,128)(2,1)S(1)}, bf16[4,24576]{1,0:T(4,128)(2,1)S(1)}, u32[]{:S(2)}, u32[]{:S(2)}) %collective-permute-start.3) | collective-permute-done | bytes 196640 | tf_op jit(solution)/shard_map/ppermute | solution.py:185
  652.9 0.1 bitcast_add_fusion
  653.0 11.0 %grad_inputs.3.refs_0_ = bf16[64,512,256]{2,1,0:T(8,128)(2,1)} custom-call(bf16[512,512]{1,0:T(8,128)(2,1)} %bitcast.22, bf16[8,64,64,128]{3,2,1,0:T(8,128)(2,1)} %all-to-all-done.3.g_ref), custom_call_target="tpu_custom_call" | custom-call | flops 4294967296 | bytes 16777216 | tf_op jit(solution)/shard_map/grad_inputs/pallas_call | solution.py:160
  664.0 1.1 broadcast_in_dim.3.start_ref
  665.1 9.1 %grad_right.2.start_ref = f32[512,512]{1,0:T(8,128)} custom-call(bf16[8,64,64,128]{3,2,1,0:T(8,128)(2,1)} %all-to-all-done.3.g_ref, bf16[64,512,256]{2,1,0:T(8,128)(2,1)} %x_ref.7, f32[512,512]{1,0:T(8,128)} %broadcast_in_dim.3.start_ref), custom_call_target="tpu_custom_call" | custom-call | flops 4294967296 | bytes 16777216 | tf_op jit(solution)/shard_map/grad_right/pallas_call | solution.py:107
  674.2 88.0 %all-to-all-done.2.g_ref = bf16[8,64,64,128]{3,2,1,0:T(8,128)(2,1)} async-done(((bf16[8,64,64,128]{3,2,1,0:T(8,128)(2,1)}), bf16[8,64,64,128]{3,2,1,0:T(8,128)(2,1)}, u32[]{:S(2)}, u32[]{:S(2)}) %all-to-all-start.2) | async-done | bytes 8388640 | tf_op jit(solution)/shard_map/all_to_all | solution.py:200
  762.2 8.8 %grad_right.3 = bf16[512,512]{1,0:T(8,128)(2,1)} custom-call(bf16[8,64,64,128]{3,2,1,0:T(8,128)(2,1)} %all-to-all-done.2.g_ref, bf16[64,512,256]{2,1,0:T(8,128)(2,1)} %x_ref.7, f32[512,512]{1,0:T(8,128)} %grad_right.2.start_ref), custom_call_target="tpu_custom_call" | custom-call | flops 4294967296 | bytes 16777216 | tf_op jit(solution)/shard_map/grad_right/pallas_call | solution.py:107
  771.0 6.2 grad_inputs.4.refs_0_
  777.2 0.1 convert_element_type.25
  777.3 0.3 constant_dynamic-slice_fusion.2
  777.6 0.1 collective-permute-start.4
  777.7 3.2 collective-permute-start.5
  780.9 1.1 collective-permute-start.6
  782.1 6.2 grad_inputs.5
  788.3 4.0 all-to-all-start.4
  792.3 0.0 collective-permute-done.4
  792.3 0.0 collective-permute-done.5
  792.3 0.0 collective-permute-done.6
  792.3 0.2 convert_add_fusion
  792.6 0.2 slice_reduce_fusion
  792.8 0.6 reshape.60
  793.4 0.1 slice_reduce_fusion.1
  793.5 0.6 reshape.59
  794.1 13.7 %all-to-all-done.4 = bf16[32,16,512]{2,1,0:T(8,128)(2,1)S(1)} async-done(((bf16[32,16,512]{2,1,0:T(8,128)(2,1)}), bf16[32,16,512]{2,1,0:T(8,128)(2,1)S(1)}, u32[]{:S(2)}, u32[]{:S(2)}) %all-to-all-start.4) | async-done | bytes 524320 | tf_op jit(solution)/shard_map/all_to_all | solution.py:346
  807.8 0.7 convert_reduce_fusion
  (8 shorter events, 0.0 us)
Async XLA Ops:
  0.6 205.9 %copy-start = (bf16[512,256]{1,0:T(8,128)(2,1)S(1)}, bf16[512,256]{1,0:T(8,128)(2,1)}, u32[]{:S(2)}) copy-start(bf16[512,256]{1,0:T(8,128)(2,1)} %param.10) | copy-start | bytes 786436
  9.8 190.5 %all-to-all-start.1 = ((bf16[8,64,64,128]{3,2,1,0:T(8,128)(2,1)}), bf16[8,64,64,128]{3,2,1,0:T(8,128)(2,1)}, u32[]{:S(2)}, u32[]{:S(2)}) async-start(bf16[8,64,64,128]{3,2,1,0:T(8,128)(2,1)} %section_one.3), calls=%async_computation.1 | async-start | bytes 16777216 | tf_op jit(solution)/shard_map/all_to_all | solution.py:200
  26.2 179.3 %copy-start.4 = (bf16[512,512]{1,0:T(8,128)(2,1)S(1)}, bf16[512,512]{1,0:T(8,128)(2,1)}, u32[]{:S(2)}) copy-start(bf16[512,512]{1,0:T(8,128)(2,1)} %left_ref.3) | copy-start | bytes 1572868
  200.3 187.2 %all-to-all-start = ((bf16[8,64,64,128]{3,2,1,0:T(8,128)(2,1)}), bf16[8,64,64,128]{3,2,1,0:T(8,128)(2,1)}, u32[]{:S(2)}, u32[]{:S(2)}) async-start(bf16[8,64,64,128]{3,2,1,0:T(8,128)(2,1)} %section_one.2), calls=%async_computation | async-start | bytes 16777216 | tf_op jit(solution)/shard_map/all_to_all | solution.py:200
  387.5 187.1 %all-to-all-start.3 = ((bf16[8,64,64,128]{3,2,1,0:T(8,128)(2,1)}), bf16[8,64,64,128]{3,2,1,0:T(8,128)(2,1)}, u32[]{:S(2)}, u32[]{:S(2)}) async-start(bf16[8,64,64,128]{3,2,1,0:T(8,128)(2,1)} %get-tuple-element.30), calls=%async_computation.3 | async-start | bytes 16777216 | tf_op jit(solution)/shard_map/all_to_all | solution.py:200
  392.7 33.4 %copy-start.3 = (f32[512,512]{1,0:T(8,128)S(1)}, f32[512,512]{1,0:T(8,128)}, u32[]{:S(2)}) copy-start(f32[512,512]{1,0:T(8,128)} %get-tuple-element.36) | copy-start | bytes 3145732
  392.7 36.9 %copy-start.5 = (f32[512,128]{1,0:T(8,128)S(1)}, f32[512,128]{1,0:T(8,128)}, u32[]{:S(2)}) copy-start(f32[512,128]{1,0:T(8,128)} %get-tuple-element.38) | copy-start | bytes 786436
  427.7 152.3 %collective-permute-start = (f32[1,8,16,512]{3,2,1,0:T(8,128)S(1)}, f32[1,8,16,512]{3,2,1,0:T(8,128)S(1)}, u32[]{:S(2)}, u32[]{:S(2)}) collective-permute-start(f32[1,8,16,512]{3,2,1,0:T(8,128)S(1)} %get-tuple-element.44), channel_id=1, source_target_pairs={{0,1},{1,0},{2,3},{3,2},{4,5},{5,4},{6,7},{7,6},{8,9},{9,8},{10,11... | collective-permute-start | bytes 786440 | tf_op jit(solution)/shard_map/ppermute | solution.py:185
  427.7 152.3 %collective-permute-start.1 = (f32[1,8,16,512]{3,2,1,0:T(8,128)S(1)}, f32[1,8,16,512]{3,2,1,0:T(8,128)S(1)}, u32[]{:S(2)}, u32[]{:S(2)}) collective-permute-start(f32[1,8,16,512]{3,2,1,0:T(8,128)S(1)} %get-tuple-element.46), channel_id=1, source_target_pairs={{0,2},{1,3},{2,0},{3,1},{4,6},{5,7},{6,4},{7,5},{8,10},{9,11},{10,... | collective-permute-start | bytes 786440 | tf_op jit(solution)/shard_map/ppermute | solution.py:185
  429.3 150.7 %collective-permute-start.2 = (f32[1,8,16,512]{3,2,1,0:T(8,128)S(1)}, f32[1,8,16,512]{3,2,1,0:T(8,128)}, u32[]{:S(2)}, u32[]{:S(2)}) collective-permute-start(f32[1,8,16,512]{3,2,1,0:T(8,128)S(1)} %get-tuple-element.45), channel_id=1, source_target_pairs={{0,3},{1,2},{2,1},{3,0},{4,7},{5,6},{6,5},{7,4},{8,11},{9,10},{10,... | collective-permute-start | bytes 786440 | tf_op jit(solution)/shard_map/ppermute | solution.py:185
  574.6 9.0 %copy-start.2 = (bf16[512,512]{1,0:T(8,128)(2,1)S(1)}, bf16[512,512]{1,0:T(8,128)(2,1)}, u32[]{:S(2)}) copy-start(bf16[512,512]{1,0:T(8,128)(2,1)} %w_ref.3) | copy-start | bytes 1572868
  574.6 10.0 %copy-start.6 = (f32[64,128]{1,0:T(8,128)S(1)}, f32[64,128]{1,0:T(8,128)}, u32[]{:S(2)}) copy-start(f32[64,128]{1,0:T(8,128)} %get-tuple-element.28) | copy-start | bytes 98308
  574.6 10.0 %copy-start.7 = (f32[64,128]{1,0:T(8,128)S(1)}, f32[64,128]{1,0:T(8,128)}, u32[]{:S(2)}) copy-start(f32[64,128]{1,0:T(8,128)} %get-tuple-element.29) | copy-start | bytes 98308
  574.6 187.6 %all-to-all-start.2 = ((bf16[8,64,64,128]{3,2,1,0:T(8,128)(2,1)}), bf16[8,64,64,128]{3,2,1,0:T(8,128)(2,1)}, u32[]{:S(2)}, u32[]{:S(2)}) async-start(bf16[8,64,64,128]{3,2,1,0:T(8,128)(2,1)} %get-tuple-element.27), calls=%async_computation.2 | async-start | bytes 16777216 | tf_op jit(solution)/shard_map/all_to_all | solution.py:200
  581.9 70.9 %collective-permute-start.3 = (bf16[4,24576]{1,0:T(4,128)(2,1)S(1)}, bf16[4,24576]{1,0:T(4,128)(2,1)S(1)}, u32[]{:S(2)}, u32[]{:S(2)}) collective-permute-start(bf16[4,24576]{1,0:T(4,128)(2,1)S(1)} %fusion.2), channel_id=1, source_target_pairs={{0,4},{4,0},{8,12},{12,8},{16,20},{20,16},{24,28},{28,24},{1,5},{5... | collective-permute-start | bytes 589832 | tf_op jit(solution)/shard_map/ppermute | solution.py:185
  777.6 14.7 %collective-permute-start.4 = (bf16[1,24576]{1,0:T(2,128)(2,1)S(1)}, bf16[1,24576]{1,0:T(2,128)(2,1)S(1)}, u32[]{:S(2)}, u32[]{:S(2)}) collective-permute-start(bf16[1,24576]{1,0:T(2,128)(2,1)S(1)} %get-tuple-element.47), channel_id=1, source_target_pairs={{0,8},{4,12},{8,0},{12,4},{16,24},{20,28},{24,16},{28,20},{1,9},{5... | collective-permute-start | bytes 147464 | tf_op jit(solution)/shard_map/ppermute | solution.py:185
  777.7 14.6 %collective-permute-start.5 = (bf16[1,24576]{1,0:T(2,128)(2,1)S(1)}, bf16[1,24576]{1,0:T(2,128)(2,1)S(1)}, u32[]{:S(2)}, u32[]{:S(2)}) collective-permute-start(bf16[1,24576]{1,0:T(2,128)(2,1)S(1)} %get-tuple-element.49), channel_id=1, source_target_pairs={{0,16},{4,20},{8,24},{12,28},{16,0},{20,4},{24,8},{28,12},{1,17},{... | collective-permute-start | bytes 147464 | tf_op jit(solution)/shard_map/ppermute | solution.py:185
  780.9 11.4 %collective-permute-start.6 = (bf16[1,24576]{1,0:T(2,128)(2,1)S(1)}, bf16[1,24576]{1,0:T(2,128)(2,1)S(1)}, u32[]{:S(2)}, u32[]{:S(2)}) collective-permute-start(bf16[1,24576]{1,0:T(2,128)(2,1)S(1)} %get-tuple-element.48), channel_id=1, source_target_pairs={{0,24},{4,28},{8,16},{12,20},{16,8},{20,12},{24,0},{28,4},{1,25},{... | collective-permute-start | bytes 147464 | tf_op jit(solution)/shard_map/ppermute | solution.py:185
  782.1 26.5 %copy-start.1 = (bf16[512,256]{1,0:T(8,128)(2,1)S(1)}, bf16[512,256]{1,0:T(8,128)(2,1)}, u32[]{:S(2)}) copy-start(bf16[512,256]{1,0:T(8,128)(2,1)} %param.10) | copy-start | bytes 786436
  788.3 19.5 %all-to-all-start.4 = ((bf16[32,16,512]{2,1,0:T(8,128)(2,1)}), bf16[32,16,512]{2,1,0:T(8,128)(2,1)S(1)}, u32[]{:S(2)}, u32[]{:S(2)}) async-start(bf16[32,16,512]{2,1,0:T(8,128)(2,1)} %bitcast.9), calls=%async_computation.4 | async-start | bytes 1048576 | tf_op jit(solution)/shard_map/all_to_all | solution.py:346
